TPU v7x, 256 devices: a whole 4x4x8 slice. The times are simulated.
256 devices in a mesh: grp: 4 (over y), dev: 64 (over x, z, core).
Axes of the slice: x: 4, y: 4, z: 8, core: 2. Of those that a mesh axis runs over, the one named last changes fastest.
Arguments:
- features: bfloat16 [32768, 768], P(('grp', 'dev')), may hold values from -6 to 6
- neighbours: int32 [32768, 25], P(('grp', 'dev')), may hold values from 0 to 32767, as said below
- neighbour_mask: int32 [32768, 25], P(('grp', 'dev')), may hold values from 0 to 1, as said below
- layer2_position: int32 [32768], P(('grp', 'dev')), may hold values from 0 to 32767, as said below
- self_weight1: bfloat16 [768, 1024], replicated, may hold values from -0.21875 to 0.21875
- neigh_weight1: bfloat16 [768, 1024], replicated, may hold values from -0.4375 to 0.4375
- self_weight2: bfloat16 [1024, 1024], replicated, may hold values from -0.1875 to 0.1875
- neigh_weight2: bfloat16 [1024, 1024], replicated, may hold values from -0.375 to 0.375
Outputs:
- embeddings: bfloat16 [32768, 1024], P(('grp', 'dev'))
Inputs may be any that keep to these rules, and one draw needn't show every extreme that they name: `neighbours`: node n is owned by device n // 128 (devices numbered grp-major). Slot 0 of every node is valid. Of one device's nodes, at most 6 valid slots name nodes of any one other device, and exactly 6 do for some other device; 765 slots of one device name other devices' nodes, all of them valid. Invalid slots hold ids of the device's own nodes. `neighbour_mask`: values 0 or 1; 1 at slot 0 and wherever the neighbour lies on another device. A permutation of the nodes; a node's new owner, layer2_position // 128, is in the same group as its old one. One device hands exactly 4 nodes to each owner of its group whose index within the group differs from its own by an even number, and none to the others.
All inputs are finite; a program needn't handle non-finite values.
Results may differ from a plain program's by a relative error of at most 0.0052.
Values may be sent and summed in bfloat16 or wider, within the bound.
A program may use at most 64 MiB of HBM per device.

v0:
```python
import jax
import jax.numpy as jnp
from jax import lax
from jax.sharding import PartitionSpec as P

CAP = 6


def slot_of(owners, usable, peer_count, capacity):
    item_count = owners.shape[0]
    sort_key = jnp.where(usable, owners, peer_count)
    ordering = jnp.argsort(sort_key, stable=True)
    per_owner = jnp.zeros((peer_count + 1,), jnp.int32).at[sort_key].add(1)
    starts = jnp.cumsum(per_owner) - per_owner
    ranked = jnp.arange(item_count, dtype=jnp.int32) - starts[sort_key[ordering]]
    ranks = jnp.zeros((item_count,), jnp.int32).at[ordering].set(ranked)
    return jnp.where(usable, owners * capacity + ranks, peer_count * capacity)


def serve_rows(source, asked_rows, asked_live):
    picked = source[asked_rows]
    return jnp.where(asked_live[..., None], picked, jnp.zeros_like(picked))


def mean_of(source, answer, adjacency, degree_count):
    width = source.shape[1]
    lookup = jnp.concatenate([source, answer.reshape(-1, width)], axis=0)
    summed = jnp.dot(adjacency, lookup, preferred_element_type=jnp.float32)
    return (summed / degree_count[:, None]).astype(jnp.bfloat16)


def body(
    features,
    neighbours,
    neighbour_mask,
    layer2_position,
    self_weight1,
    neigh_weight1,
    self_weight2,
    neigh_weight2,
):
    row_count, degree = neighbours.shape
    groups = lax.axis_size("grp")
    members = lax.axis_size("dev")
    peer_count = groups * members
    own_index = lax.axis_index("grp") * members + lax.axis_index("dev")
    flat_ids = neighbours.reshape(-1)
    usable = neighbour_mask.reshape(-1) > 0
    owners = flat_ids // row_count
    local_row = flat_ids % row_count
    remote = usable & (owners != own_index)
    slots = slot_of(owners, remote, peer_count, CAP)
    request = jnp.full((peer_count * CAP + 1,), -1, jnp.int32).at[slots].set(local_row)
    request = request[:-1].reshape(groups, members, CAP)
    asked = lax.all_to_all(
        lax.all_to_all(request, "grp", split_axis=0, concat_axis=0, tiled=True),
        "dev",
        split_axis=1,
        concat_axis=1,
        tiled=True,
    )
    asked_live = asked >= 0
    asked_rows = jnp.maximum(asked, 0)
    lookup_rows = row_count + peer_count * CAP
    table_index = jnp.where(remote, row_count + slots, jnp.where(usable, local_row, 0))
    table_index = jnp.minimum(table_index, lookup_rows - 1)
    node_index = jnp.arange(row_count * degree, dtype=jnp.int32) // degree
    slot_weight = jnp.where(usable, 1.0, 0.0).astype(jnp.bfloat16)
    adjacency = (
        jnp.zeros((row_count, lookup_rows), jnp.bfloat16)
        .at[node_index, table_index]
        .add(slot_weight)
    )
    degree_count = jnp.sum(neighbour_mask, axis=1).astype(jnp.float32)
    reply_first = serve_rows(features, asked_rows, asked_live)
    answer_first = lax.all_to_all(
        lax.all_to_all(reply_first, "grp", split_axis=0, concat_axis=0, tiled=True),
        "dev",
        split_axis=1,
        concat_axis=1,
        tiled=True,
    )
    own_first = jnp.dot(features, self_weight1, preferred_element_type=jnp.float32)
    mean_first = mean_of(features, answer_first, adjacency, degree_count)
    hidden = jax.nn.relu(
        own_first + jnp.dot(mean_first, neigh_weight1, preferred_element_type=jnp.float32)
    ).astype(jnp.bfloat16)
    reply_second = serve_rows(hidden, asked_rows, asked_live)
    answer_second = lax.all_to_all(
        lax.all_to_all(reply_second, "grp", split_axis=0, concat_axis=0, tiled=True),
        "dev",
        split_axis=1,
        concat_axis=1,
        tiled=True,
    )
    own_second = jnp.dot(hidden, self_weight2, preferred_element_type=jnp.float32)
    mean_second = mean_of(hidden, answer_second, adjacency, degree_count)
    final = (
        own_second + jnp.dot(mean_second, neigh_weight2, preferred_element_type=jnp.float32)
    ).astype(jnp.bfloat16)
    width = final.shape[1]
    capacity_two = 2 * row_count // members
    target = layer2_position // row_count % members
    every_row = jnp.ones((row_count,), jnp.bool_)
    moves = slot_of(target, every_row, members, capacity_two)
    outgoing = (
        jnp.zeros((members * capacity_two + 1, width), jnp.bfloat16)
        .at[moves]
        .set(final)[:-1]
        .reshape(members, capacity_two, width)
    )
    places = (
        jnp.full((members * capacity_two + 1,), -1, jnp.int32)
        .at[moves]
        .set(layer2_position % row_count)[:-1]
        .reshape(members, capacity_two)
    )
    arrived, arrived_places = (
        lax.all_to_all(outgoing, "dev", split_axis=0, concat_axis=0, tiled=True),
        lax.all_to_all(places, "dev", split_axis=0, concat_axis=0, tiled=True),
    )
    flat_places = arrived_places.reshape(-1)
    landing = jnp.where(flat_places >= 0, flat_places, row_count)
    embeddings = (
        jnp.zeros((row_count + 1, width), jnp.bfloat16)
        .at[landing]
        .set(arrived.reshape(-1, width))[:-1]
    )
    return embeddings


def solution(mesh):
    return jax.shard_map(
        body,
        mesh=mesh,
        in_specs=(
            P(("grp", "dev"), None),
            P(("grp", "dev"), None),
            P(("grp", "dev"), None),
            P(("grp", "dev")),
            P(),
            P(),
            P(),
            P(),
        ),
        out_specs=P(("grp", "dev"), None),
        check_vma=False,
    )
```

profile of v0, /device:TPU:1, one launch (start us, length us, event | category | flops | bytes accessed | tf_op | source)
XLA Modules:
  0.0 454.2 jit_solution(8724098376298741150)
XLA Ops:
  2.8 23.3 %scatter_custom_fusion.3 = s32[257]{0:T(512)S(1)} fusion(s32[3200]{0:T(1024)S(1)} %fusion.36, s32[3200]{0:T(1024)S(1)} %ne.122, s32[]{:T(128)} %constant.64.clone.1), kind=kCustom, calls=%fused_computation.106 | custom fusion | flops 3200 | bytes 1032 | tf_op jit(solution)/shard_map/scatter-add | solution.py:13
  26.8 5.8 %sort.35 = (s32[3200]{0:T(1024)}, s32[3200]{0:T(1024)S(1)}) sort(s32[3200]{0:T(1024)S(1)} %get-tuple-element.14, s32[3200]{0:T(1024)S(1)} %iota.21), dimensions={0}, to_apply=%region_5.6 | sort | flops 38400 | bytes 51200 | tf_op jit(solution)/shard_map/jit(argsort)/sort | solution.py:12
  32.6 16.9 %gather_fusion.2 = s32[3200]{0:T(1024)S(1)} fusion(s32[3200]{0:T(1024)S(1)} %get-tuple-element.14, s32[4096]{0:T(1024)S(1)} %pad_clamp_fusion.1), kind=kCustom, calls=%fused_computation.2 | custom fusion | bytes 38400 | tf_op jit(solution)/shard_map/gather | solution.py:15
  49.6 19.2 %gather_fusion.3 = s32[3200]{0:T(1024)S(1)} fusion(s32[257]{0:T(512)S(1)} %slice_subtract_fusion, s32[4096]{0:T(1024)S(1)} %pad_clamp_fusion), kind=kCustom, calls=%fused_computation.3 | custom fusion | bytes 38400 | tf_op jit(solution)/shard_map/gather | solution.py:15
  68.9 15.8 %scatter_custom_fusion.4 = s32[3200]{0:T(1024)S(1)} fusion(s32[3200]{0:T(1024)S(1)} %compare_select_fusion.5, s32[3200]{0:T(1024)S(1)} %iota_subtract_fusion, s32[]{:T(128)} %constant.64.clone.1), kind=kCustom, calls=%fused_computation.79 | custom fusion | bytes 12804 | tf_op jit(solution)/shard_map/scatter | solution.py:16
  84.8 15.8 %scatter_custom_fusion.5 = s32[1537]{0:T(1024)S(1)} fusion(s32[3200]{0:T(1024)S(1)} %get-tuple-element.11, s32[3200]{0:T(1024)S(1)} %get-tuple-element.13, s32[]{:T(128)} %constant.59.clone.1), kind=kCustom, calls=%fused_computation.88 | custom fusion | bytes 6152 | tf_op jit(solution)/shard_map/scatter | solution.py:53
  100.9 9.0 %all_to_all.44 = s32[4,1,384]{2,1,0:T(1,128)S(1)} all-to-all(s32[4,1,384]{2,1,0:T(1,128)S(1)} %reshape.449), channel_id=1, replica_groups=mesh['grp'=4,'dev'=64] {'grp'}, dimensions={0} | all-to-all | bytes 12288 | tf_op jit(solution)/shard_map/all_to_all | solution.py:56
  111.3 23.7 %all_to_all.45 = s32[4,64,6]{2,0,1:T(4,128)S(1)} all-to-all(s32[4,64,6]{2,0,1:T(4,128)S(1)} %copy.39), channel_id=1, replica_groups=mesh['grp'=4,'dev'=64] {'dev'}, dimensions={1} | all-to-all | bytes 12288 | tf_op jit(solution)/shard_map/all_to_all | solution.py:55
  135.5 5.6 %gather_fusion.4 = bf16[1536,768]{1,0:T(8,128)(2,1)} fusion(bf16[128,768]{1,0:T(8,128)(2,1)S(1)} %copy-done.1, s32[2048]{0:T(1024)S(1)} %pad_clamp_fusion.2), kind=kCustom, calls=%fused_computation.4 | custom fusion | bytes 4724736 | tf_op jit(solution)/shard_map/gather | solution.py:21
  141.1 5.0 %reshape.321 = bf16[4,64,6,768]{3,2,1,0:T(8,128)(2,1)} reshape(bf16[1536,768]{1,0:T(8,128)(2,1)} %gather_fusion.4) | data formatting | bytes 4718592 | tf_op jit(solution)/shard_map/gather | solution.py:21
  148.9 31.8 %all_to_all.46 = bf16[4,64,6,768]{3,1,2,0:T(8,128)(2,1)S(1)} all-to-all(bf16[4,64,6,768]{3,1,2,0:T(8,128)(2,1)S(1)} %copy.44), channel_id=1, replica_groups=mesh['grp'=4,'dev'=64] {'grp'}, dimensions={0} | all-to-all | bytes 4718592 | tf_op jit(solution)/shard_map/all_to_all | solution.py:77
  184.0 6.3 %all-to-all-start.4 = ((bf16[4,64,6,768]{3,0,2,1:T(4,128)(2,1)}), bf16[4,64,6,768]{3,0,2,1:T(4,128)(2,1)}, u32[]{:S(2)}, u32[]{:S(2)}) async-start(bf16[4,64,6,768]{3,0,2,1:T(4,128)(2,1)} %copy.45), calls=%async_computation.4 | async-start | bytes 4718592 | tf_op jit(solution)/shard_map/all_to_all | solution.py:76
  190.6 29.1 %scatter_custom_fusion.8 = bf16[212992]{0:T(1024)(128)(2,1)S(1)} fusion(s32[3200]{0:T(1024)S(1)} %broadcast_select_fusion.2, bf16[3200]{0:T(1024)(128)(2,1)S(1)} %select_convert_fusion, bf16[]{:T(256)} %constant.58.clone.1), kind=kCustom, calls=%fused_computation.37 | custom fusion | flops 3200 | bytes 425986
  222.0 24.9 %all-to-all-done.4 = bf16[4,64,6,768]{3,0,2,1:T(4,128)(2,1)} async-done(((bf16[4,64,6,768]{3,0,2,1:T(4,128)(2,1)}), bf16[4,64,6,768]{3,0,2,1:T(4,128)(2,1)}, u32[]{:S(2)}, u32[]{:S(2)}) %all-to-all-start.4) | async-done | bytes 2359328 | tf_op jit(solution)/shard_map/all_to_all | solution.py:76
  250.7 5.1 %reshape.280 = bf16[1536,768]{1,0:T(8,128)(2,1)} reshape(bf16[4,64,6,768]{3,2,1,0:T(8,128)(2,1)} %copy.46) | data formatting | bytes 4718592 | tf_op jit(solution)/shard_map/reshape | solution.py:27
  258.9 5.9 %gather_fusion.5 = bf16[1536,1024]{1,0:T(8,128)(2,1)} fusion(bf16[128,1024]{1,0:T(8,128)(2,1)S(1)} %fusion.9, s32[2048]{0:T(1024)S(1)} %pad_clamp_fusion.2), kind=kCustom, calls=%fused_computation.5 | custom fusion | bytes 6297600 | tf_op jit(solution)/shard_map/gather | solution.py:21
  264.7 6.2 %reshape.329 = bf16[4,64,6,1024]{3,2,1,0:T(8,128)(2,1)} reshape(bf16[1536,1024]{1,0:T(8,128)(2,1)} %gather_fusion.5) | data formatting | bytes 6291456 | tf_op jit(solution)/shard_map/gather | solution.py:21
  275.3 39.9 %all_to_all.47 = bf16[4,64,6,1024]{3,1,2,0:T(8,128)(2,1)S(1)} all-to-all(bf16[4,64,6,1024]{3,1,2,0:T(8,128)(2,1)S(1)} %copy.48), channel_id=1, replica_groups=mesh['grp'=4,'dev'=64] {'grp'}, dimensions={0} | all-to-all | bytes 6291456 | tf_op jit(solution)/shard_map/all_to_all | solution.py:90
  319.2 6.7 %all-to-all-start.6 = ((bf16[4,64,6,1024]{3,0,2,1:T(4,128)(2,1)}), bf16[4,64,6,1024]{3,0,2,1:T(4,128)(2,1)}, u32[]{:S(2)}, u32[]{:S(2)}) async-start(bf16[4,64,6,1024]{3,0,2,1:T(4,128)(2,1)} %copy.49), calls=%async_computation.6 | async-start | bytes 6291456 | tf_op jit(solution)/shard_map/all_to_all | solution.py:89
  336.1 63.2 %all-to-all-done.6 = bf16[4,64,6,1024]{3,0,2,1:T(4,128)(2,1)} async-done(((bf16[4,64,6,1024]{3,0,2,1:T(4,128)(2,1)}), bf16[4,64,6,1024]{3,0,2,1:T(4,128)(2,1)}, u32[]{:S(2)}, u32[]{:S(2)}) %all-to-all-start.6) | async-done | bytes 3145760 | tf_op jit(solution)/shard_map/all_to_all | solution.py:89
  399.3 6.1 %all-to-all-start = ((s32[64,1,4]{2,1,0:T(1,128)}), s32[64,1,4]{2,1,0:T(1,128)S(1)}, u32[]{:S(2)}, u32[]{:S(2)}) async-start(s32[64,1,4]{2,1,0:T(1,128)} %bitcast.3), calls=%async_computation | async-start | bytes 65536 | tf_op jit(solution)/shard_map/all_to_all | solution.py:120
  410.4 6.3 %reshape.281 = bf16[1536,1024]{1,0:T(8,128)(2,1)} reshape(bf16[4,64,6,1024]{3,2,1,0:T(8,128)(2,1)} %copy.50) | data formatting | bytes 6291456 | tf_op jit(solution)/shard_map/reshape | solution.py:27
  423.7 10.3 %all-to-all-start.7 = ((bf16[64,4,1024]{2,1,0:T(4,128)(2,1)}), bf16[64,4,1024]{2,1,0:T(4,128)(2,1)S(1)}, u32[]{:S(2)}, u32[]{:S(2)}) async-start(bf16[64,4,1024]{2,1,0:T(4,128)(2,1)} %reshape.282), calls=%async_computation.7 | async-start | bytes 1048576 | tf_op jit(solution)/shard_map/all_to_all | solution.py:119
  435.4 16.0 %all-to-all-done.7 = bf16[64,4,1024]{2,1,0:T(4,128)(2,1)S(1)} async-done(((bf16[64,4,1024]{2,1,0:T(4,128)(2,1)}), bf16[64,4,1024]{2,1,0:T(4,128)(2,1)S(1)}, u32[]{:S(2)}, u32[]{:S(2)}) %all-to-all-start.7) | async-done | bytes 524320 | tf_op jit(solution)/shard_map/all_to_all | solution.py:119
  (103 shorter events, 55.4 us)
Async XLA Ops:
  0.0 335.7 %copy-start = (bf16[1024,1024]{1,0:T(8,128)(2,1)S(1)}, bf16[1024,1024]{1,0:T(8,128)(2,1)}, u32[]{:S(2)}) copy-start(bf16[1024,1024]{1,0:T(8,128)(2,1)} %param.14) | copy-start | bytes 6291460
  68.8 66.6 %copy-start.1 = (bf16[128,768]{1,0:T(8,128)(2,1)S(1)}, bf16[128,768]{1,0:T(8,128)(2,1)}, u32[]{:S(2)}) copy-start(bf16[128,768]{1,0:T(8,128)(2,1)} %param.8) | copy-start | bytes 589828
  184.0 6.3 %copy-start.2 = (s32[128,25]{0,1:T(8,128)S(1)}, s32[128,25]{0,1:T(8,128)}, u32[]{:S(2)}) copy-start(s32[128,25]{0,1:T(8,128)} %param.10) | copy-start | bytes 38404
  184.0 6.4 %copy-start.4 = (s32[2]{0:T(128)S(1)}, s32[2]{0:T(128)}, u32[]{:S(2)}) copy-start(s32[2]{0:T(128)} %constant.134) | copy-start | bytes 28
  184.0 6.5 %copy-start.3 = (s32[2]{0:T(128)S(1)}, s32[2]{0:T(128)}, u32[]{:S(2)}) copy-start(s32[2]{0:T(128)} %constant.137) | copy-start | bytes 28
  184.0 62.9 %all-to-all-start.4 = ((bf16[4,64,6,768]{3,0,2,1:T(4,128)(2,1)}), bf16[4,64,6,768]{3,0,2,1:T(4,128)(2,1)}, u32[]{:S(2)}, u32[]{:S(2)}) async-start(bf16[4,64,6,768]{3,0,2,1:T(4,128)(2,1)} %copy.45), calls=%async_computation.4 | async-start | bytes 4718592 | tf_op jit(solution)/shard_map/all_to_all | solution.py:76
  319.2 6.7 %copy-start.5 = (s32[128]{0:T(128)S(1)}, s32[128]{0:T(128)}, u32[]{:S(2)}) copy-start(s32[128]{0:T(128)} %param.11) | copy-start | bytes 1540
  319.2 80.1 %all-to-all-start.6 = ((bf16[4,64,6,1024]{3,0,2,1:T(4,128)(2,1)}), bf16[4,64,6,1024]{3,0,2,1:T(4,128)(2,1)}, u32[]{:S(2)}, u32[]{:S(2)}) async-start(bf16[4,64,6,1024]{3,0,2,1:T(4,128)(2,1)} %copy.49), calls=%async_computation.6 | async-start | bytes 6291456 | tf_op jit(solution)/shard_map/all_to_all | solution.py:89
  399.3 24.4 %all-to-all-start = ((s32[64,1,4]{2,1,0:T(1,128)}), s32[64,1,4]{2,1,0:T(1,128)S(1)}, u32[]{:S(2)}, u32[]{:S(2)}) async-start(s32[64,1,4]{2,1,0:T(1,128)} %bitcast.3), calls=%async_computation | async-start | bytes 65536 | tf_op jit(solution)/shard_map/all_to_all | solution.py:120
  423.7 27.7 %all-to-all-start.7 = ((bf16[64,4,1024]{2,1,0:T(4,128)(2,1)}), bf16[64,4,1024]{2,1,0:T(4,128)(2,1)S(1)}, u32[]{:S(2)}, u32[]{:S(2)}) async-start(bf16[64,4,1024]{2,1,0:T(4,128)(2,1)} %reshape.282), calls=%async_computation.7 | async-start | bytes 1048576 | tf_op jit(solution)/shard_map/all_to_all | solution.py:119
where the time goes:
time: 463 us; the launch traced here: 454 us
  local copies, waits for them, and re-layouts  136 us (29%)
  blocking collectives  104 us (22%)
  waiting for transfers between devices  104 us (22%)
  other arithmetic  70.3 us (15%)
  starting transfers between devices  29.3 us (6%)
  matrix products  9.57 us (2%)
    all_to_all x1, waiting for transfers between devices, body(): lax.all_to_all(lax.all_to_all(reply_second, 'grp', split_axis=0, concat_a...  63.2 us
    all_to_all x1, blocking collectives, body(): lax.all_to_all(reply_second, 'grp', split_axis=0, concat_axis=0, tiled=True)  39.9 us
    all_to_all x1, blocking collectives, body(): lax.all_to_all(reply_first, 'grp', split_axis=0, concat_axis=0, tiled=True)  31.8 us
    unnamed x4, other arithmetic  29.3 us
    all_to_all x1, waiting for transfers between devices, body(): lax.all_to_all(lax.all_to_all(reply_first, 'grp', split_axis=0, concat_ax...  24.9 us
    scatter-add x2, other arithmetic, slot_of(): per_owner = jnp.zeros((peer_count + 1,), jnp.int32).at[sort_key].add(1)  24.7 us
    all_to_all x1, blocking collectives, body(): lax.all_to_all(lax.all_to_all(request, 'grp', split_axis=0, concat_axis=0...  23.7 us
    gather x4, local copies, waits for them, and re-layouts, serve_rows(): picked = source[asked_rows]  22.7 us
  transfers between devices with their start and end apart: 4, of which 3 were waited for; matrix products, arithmetic and copies ran while one was open for 13% of the time, Pallas kernels for 0%

commit v1 on v0

v1 whole, which is shorter than its diff:
```python
import jax
import jax.numpy as jnp
from jax import lax
from jax.experimental import pallas as pl
from jax.experimental.pallas import tpu as pltpu
from jax.sharding import PartitionSpec as P

NX, NZ, NC = 4, 8, 2
CAP = 6
CHUNK = 256
LANES = 128
BF = jnp.bfloat16
F32 = jnp.float32
MESH = pl.DeviceIdType.MESH


def iota(shape, dim):
    return lax.broadcasted_iota(jnp.int32, shape, dim)


def mm(a, b):
    return jnp.dot(a, b, preferred_element_type=F32)


def one_zero(cond):
    return jnp.where(cond, 1.0, 0.0).astype(BF)


def kernel(
    nb_ref,
    mk_ref,
    pos_ref,
    feat_hbm,
    ws1_hbm,
    wn1_hbm,
    ws2_hbm,
    wn2_hbm,
    out_ref,
    ws1,
    wn1,
    ws2,
    wn2,
    table,
    serve,
    ans,
    pick,
    key_ref,
    adj,
    adj2,
    loc,
    loc2,
    cnt,
    cnt2,
    slot_p,
    slot_id,
    slot_row,
    lists,
    asked,
    acc,
    hid,
    xbuf,
    arrx,
    zbuf,
    arrz,
    load_sem,
    ring_send,
    ring_recv,
    req_send,
    req_recv,
    ans_send,
    ans_recv,
    x_send,
    x_recv,
    z_send,
    z_recv,
):
    rows, degree = nb_ref.shape
    ny = lax.axis_size("grp")
    n_dev = NX * NZ * NC
    ncol = NX * ny * NC
    block = CAP * NZ
    chunk = table.shape[2]
    n1 = feat_hbm.shape[1] // chunk
    n2 = wn2.shape[0] // chunk
    hidden_width = wn2.shape[0]
    half = NZ // 2
    rank2 = rows // (NX * NZ)
    me_y = lax.axis_index("grp")
    me_dev = lax.axis_index("dev")
    me_x = me_dev // (NZ * NC)
    me_z = me_dev // NC % NZ
    me_c = me_dev % NC

    def at(x, y, z, c):
        return (y, (x * NZ + z) * NC + c)

    def ahead(d):
        return at(
            (me_x + d // (ny * NC)) % NX,
            (me_y + d // NC % ny) % ny,
            me_z,
            (me_c + d % NC) % NC,
        )

    def behind(d):
        return at(
            (me_x + NX - d // (ny * NC)) % NX,
            (me_y + ny - d // NC % ny) % ny,
            me_z,
            (me_c + NC - d % NC) % NC,
        )

    def along_z(dz):
        return at(me_x, me_y, (me_z + dz) % NZ, me_c)

    def along_x(dx):
        return at((me_x + dx) % NX, me_y, me_z, me_c)

    def drain(ref, sem):
        pltpu.make_async_copy(ref, ref, sem).wait()

    own = pl.ds(pl.multiple_of(me_z * rows, rows), rows)

    loads = []
    for k in range(n1):
        loads.append(
            pltpu.make_async_copy(
                feat_hbm.at[:, pl.ds(k * chunk, chunk)], table.at[k, own], load_sem.at[k]
            )
        )
    for k, (far, near) in enumerate(
        ((ws1_hbm, ws1), (wn1_hbm, wn1), (ws2_hbm, ws2), (wn2_hbm, wn2))
    ):
        loads.append(pltpu.make_async_copy(far, near, load_sem.at[n1 + k]))
    for load in loads:
        load.start()

    barrier = pltpu.get_barrier_semaphore()

    @pl.loop(1, NZ)
    def _(dz):
        pl.semaphore_signal(barrier, inc=1, device_id=along_z(dz), device_id_type=MESH)

    @pl.loop(1, ncol)
    def _(d):
        pl.semaphore_signal(barrier, inc=1, device_id=ahead(d), device_id_type=MESH)

    pl.semaphore_wait(barrier, NZ - 1 + ncol - 1)

    def ring_block(k, s, way, last):
        from_z = (me_z + NZ - (s - 1)) % NZ if way == 0 else (me_z + s - 1) % NZ
        if last:
            start = from_z * rows + way * (rows // 2)
            return table.at[k, pl.ds(pl.multiple_of(start, rows // 2), rows // 2)]
        return table.at[k, pl.ds(pl.multiple_of(from_z * rows, rows), rows)]

    def ring_copy(k, s, way, last):
        ref = ring_block(k, s, way, last)
        return pltpu.make_async_remote_copy(
            src_ref=ref,
            dst_ref=ref,
            send_sem=ring_send.at[k, way, s - 1],
            recv_sem=ring_recv.at[k, way, s - 1],
            device_id=along_z(1 if way == 0 else NZ - 1),
            device_id_type=MESH,
        )

    def ring_step(k, s):
        for way in range(2):

            @pl.when(s > 1)
            def _():
                drain(ring_block(k, s, way, False), ring_recv.at[k, way, s - 2])

            @pl.when(s < half)
            def _():
                ring_copy(k, s, way, False).start()

            @pl.when(s == half)
            def _():
                ring_copy(k, s, way, True).start()

    def ring_end(k):
        for way in range(2):
            drain(ring_block(k, half + 1, way, True), ring_recv.at[k, way, half - 1])

    for k in range(n1):
        loads[k].wait()
    ring_step(0, 1)

    nb = nb_ref[...]
    mk = mk_ref[...]
    owner = nb // rows
    row = nb % rows
    o_y = owner // n_dev
    o_dev = owner % n_dev
    o_x = o_dev // (NZ * NC)
    o_z = o_dev // NC % NZ
    o_c = o_dev % NC
    mine = owner == me_y * n_dev + me_dev
    valid = mk > 0
    remote = valid & jnp.logical_not(mine)
    col = (
        ((me_x + NX - o_x) % NX) * (ny * NC)
        + ((me_y + ny - o_y) % ny) * NC
        + (me_c + NC - o_c) % NC
    )
    col = jnp.where(remote, col, -4096)
    slot_id[...] = o_z * rows + row + 1
    slot_row[...] = jnp.where(valid & mine, row, -1)
    count = jnp.sum(mk.astype(F32), axis=1, keepdims=True)
    cnt[...] = jnp.broadcast_to(count, (rows, LANES))

    pack = LANES // ncol
    lane = iota((rows, LANES), 1)
    sub = iota((rows, LANES), 0)
    lower = one_zero(lane < sub)
    ones = jnp.ones((rows, LANES), BF)
    same = lane % ncol == sub % ncol
    every = one_zero(same)
    before = one_zero(same & (sub // ncol < lane // ncol))
    so_far = jnp.zeros((rows, LANES), F32)
    cols = []
    for j in range(0, degree, pack):
        members = range(j, min(j + pack, degree))
        hot = jnp.zeros((rows, LANES), jnp.bool_)
        for s in members:
            hot = hot | (col[:, s : s + 1] == lane - (s - j) * ncol)
        hot = one_zero(hot)
        totals = mm(ones, hot)
        rank = (
            mm(lower, hot)
            + mm(totals.astype(BF), before)
            + mm(so_far.astype(BF), every)
        )
        so_far = so_far + totals
        rank = rank * hot.astype(F32)
        for s in members:
            group = lane // ncol == s - j
            cols.append(jnp.sum(jnp.where(group, rank, 0.0), axis=1, keepdims=True))
    lane_s = iota((rows, degree), 1)
    ranks = jnp.zeros((rows, degree), F32)
    for s in range(degree):
        ranks = jnp.where(lane_s == s, cols[s], ranks)
    slot_p[...] = jnp.where(remote, col * block + ranks.astype(jnp.int32), -1)

    ring_step(0, 2)

    tiles = ncol * block // LANES
    lists[...] = jnp.zeros_like(lists)

    @pl.loop(0, rows // 8)
    def _(i):
        at_rows = pl.ds(pl.multiple_of(i * 8, 8), 8)
        p8 = slot_p[at_rows, :]
        id8 = slot_id[at_rows, :]
        row8 = slot_row[at_rows, :]
        lane8 = iota((8, LANES), 1)
        p_all = [jnp.broadcast_to(p8[:, s : s + 1], (8, LANES)) for s in range(degree)]
        id_all = [jnp.broadcast_to(id8[:, s : s + 1], (8, LANES)) for s in range(degree)]
        for t in range(tiles):
            got = jnp.zeros((8, LANES), jnp.int32)
            for s in range(degree):
                got = jnp.where(p_all[s] == lane8 + t * LANES, id_all[s], got)
            key_ref[at_rows, t * LANES : (t + 1) * LANES] = got
            lists[t] = lists[t] + jnp.sum(got, axis=0, keepdims=True)
        near = jnp.zeros((8, LANES), F32)
        for s in range(degree):
            near = near + jnp.where(row8[:, s : s + 1] == lane8, 1.0, 0.0)
        loc[at_rows, :] = near

    window = 8 * block // LANES

    def request(d):
        return pltpu.make_async_remote_copy(
            src_ref=lists.at[pl.ds(d // 8 * window, window)],
            dst_ref=asked.at[d],
            send_sem=req_send,
            recv_sem=req_recv,
            device_id=behind(d),
            device_id_type=MESH,
        )

    @pl.loop(1, ncol)
    def _(d):
        request(d).start()

    asked[0] = lists[0:window]
    ring_step(0, 3)

    pos = pos_ref[...]
    t_dev = pos // rows % n_dev
    t_x = t_dev // (NZ * NC)
    t_z = t_dev // NC % NZ
    target = ((t_x + NX - me_x) % NX) * NZ + (t_z + NZ - me_z) % NZ
    hot_t = iota((NX * NZ, rows), 0) == target
    ahead_of = mm(one_zero(hot_t), one_zero(sub < lane))
    rank_t = jnp.sum(jnp.where(hot_t, ahead_of, 0.0), axis=0, keepdims=True)
    place = target * rank2 + rank_t.astype(jnp.int32)
    order = place == sub
    move = one_zero(order)
    pos_b = mm(jnp.where(order, (pos % rows).astype(F32), 0.0).astype(BF), ones)
    xbuf[:, :, hidden_width:] = pos_b.astype(BF).reshape(NX, NZ * rank2, LANES)
    adj[...] = one_zero(key_ref[...] > 0)
    adj2[...] = mm(move, adj[...]).astype(BF)
    loc2[...] = mm(move, loc[...].astype(BF))
    cnt2[...] = mm(move, cnt[...].astype(BF))
    ring_step(0, 4)

    drain(asked.at[pl.ds(1, ncol - 1)], req_recv)

    @pl.loop(0, ncol)
    def _(d):
        got = asked[d]
        place = iota((block, LANES), 0) + d % 8 * block
        found = jnp.zeros((block, LANES), jnp.int32)
        for t in range(window):
            piece = jnp.broadcast_to(got[t], (block, LANES))
            found = found + jnp.where(iota((block, LANES), 1) + t * LANES == place, piece, 0)
        found = jnp.sum(found, axis=1, keepdims=True)
        hit = iota((block, NZ * rows), 1) + 1 == found
        pick[pl.ds(pl.multiple_of(d * block, block), block), :] = one_zero(hit)

    ring_end(0)

    group = 8

    def reply(k, d):
        return pltpu.make_async_remote_copy(
            src_ref=serve.at[k, d],
            dst_ref=ans.at[k, d],
            send_sem=ans_send.at[k],
            recv_sem=ans_recv.at[k],
            device_id=ahead(d),
            device_id_type=MESH,
        )

    def serve_all(first, last):
        @pl.loop(first, last)
        def _(k):
            @pl.loop(0, ncol // group)
            def _(j):
                some = pl.ds(pl.multiple_of(j * group * block, group * block), group * block)
                picked = mm(pick[some, :], table[k]).astype(BF)
                serve[k, pl.ds(j * group, group)] = picked.reshape(group, block, chunk)

                @pl.loop(0, group)
                def _(i):
                    d = j * group + i

                    @pl.when(d > 0)
                    def _():
                        reply(k, d).start()

                @pl.when(k + 1 < last)
                def _():
                    for s in range(1, half + 1):

                        @pl.when(j == (s - 1) * (ncol // group) // half)
                        def _():
                            ring_step(k + 1, s)

            ans[k, 0] = serve[k, 0]

            @pl.when(k + 1 < last)
            def _():
                ring_end(k + 1)

    def mean(k, adjacency, near, rows_own, degrees):
        drain(ans.at[k, pl.ds(1, ncol - 1)], ans_recv.at[k])
        summed = mm(adjacency[...], ans[k].reshape(ncol * block, chunk)) + mm(
            near[...].astype(BF), rows_own
        )
        return (summed / degrees[:, 0:1]).astype(BF)

    def part(k):
        return slice(k * chunk, (k + 1) * chunk)

    serve_all(0, n1)
    loads[n1].wait()
    loads[n1 + 1].wait()
    for n in range(n2):
        total = mm(table[0, own, :], ws1[part(0), part(n)])
        for k in range(1, n1):
            total = total + mm(table[k, own, :], ws1[part(k), part(n)])
        acc[:, part(n)] = total
    for k in range(n1 - 1):
        m = mean(k, adj, loc, table[k, own, :], cnt)
        for n in range(n2):
            acc[:, part(n)] += mm(m, wn1[part(k), part(n)])
    m = mean(n1 - 1, adj, loc, table[n1 - 1, own, :], cnt)
    for n in range(n2):
        total = acc[:, part(n)] + mm(m, wn1[part(n1 - 1), part(n)])
        table[n1 + n, own, :] = jnp.maximum(total, 0.0).astype(BF)
        if n == 0:
            ring_step(n1, 1)
    for s in range(2, half + 1):
        ring_step(n1, s)
    for n in range(n2):
        hid[:, part(n)] = mm(move, table[n1 + n, own, :]).astype(BF)
    ring_end(n1)
    serve_all(n1, n1 + n2)
    loads[n1 + 2].wait()
    loads[n1 + 3].wait()
    for n in range(n2):
        acc[:, part(n)] = mm(hid[...], ws2[:, part(n)])
    for k in range(n2):
        m = mean(n1 + k, adj2, loc2, table[n1 + k, own, :], cnt2)
        for n in range(n2):
            acc[:, part(n)] += mm(m, wn2[part(k), part(n)])
    xbuf[:, :, :hidden_width] = acc[...].astype(BF).reshape(NX, NZ * rank2, hidden_width)

    def x_copy(dx):
        return pltpu.make_async_remote_copy(
            src_ref=xbuf.at[dx],
            dst_ref=arrx.at[dx],
            send_sem=x_send,
            recv_sem=x_recv,
            device_id=along_x(dx),
            device_id_type=MESH,
        )

    def z_copy(dz):
        return pltpu.make_async_remote_copy(
            src_ref=zbuf.at[dz],
            dst_ref=arrz.at[dz],
            send_sem=z_send,
            recv_sem=z_recv,
            device_id=along_z(dz),
            device_id_type=MESH,
        )

    @pl.loop(1, NX)
    def _(dx):
        x_copy(dx).start()

    arrx[0] = xbuf[0]
    drain(arrx.at[pl.ds(1, NX - 1)], x_recv)
    width = hidden_width + LANES
    source = (
        sub // rank2 % NX * (NZ * rank2) + sub // (NX * rank2) * rank2 + sub % rank2
    )
    turned = mm(one_zero(source == lane), arrx[...].reshape(rows, width)).astype(BF)
    zbuf[...] = turned.reshape(NZ, NX * rank2, width)

    @pl.loop(1, NZ)
    def _(dz):
        z_copy(dz).start()

    arrz[0] = zbuf[0]
    drain(arrz.at[pl.ds(1, NZ - 1)], z_recv)
    landed = arrz[...].reshape(rows, width)
    put = one_zero(landed[:, hidden_width:].astype(F32) == lane.astype(F32))
    out_ref[...] = lax.dot_general(
        put,
        landed[:, :hidden_width],
        (((0,), (0,)), ((), ())),
        preferred_element_type=F32,
    ).astype(BF)

    drain(lists_all(asked, ncol), req_send)
    drain(xbuf.at[pl.ds(1, NX - 1)], x_send)
    drain(zbuf.at[pl.ds(1, NZ - 1)], z_send)

    @pl.loop(0, n1 + n2)
    def _(k):
        drain(serve.at[k, pl.ds(1, ncol - 1)], ans_send.at[k])
        for way in range(2):
            for s in range(1, half + 1):
                drain(ring_block(k, s, way, s == half), ring_send.at[k, way, s - 1])


def lists_all(asked, ncol):
    return asked.at[pl.ds(1, ncol - 1)]


def body(
    features,
    neighbours,
    neighbour_mask,
    layer2_position,
    self_weight1,
    neigh_weight1,
    self_weight2,
    neigh_weight2,
):
    rows, width = features.shape
    hidden = self_weight1.shape[1]
    ny = lax.axis_size("grp")
    ncol = NX * ny * NC
    block = CAP * NZ
    slots = ncol * block
    chunk = CHUNK
    n1, n2 = width // chunk, hidden // chunk
    half = NZ // 2
    degree = neighbours.shape[1]
    window = 8 * block // LANES
    rank2 = rows // (NX * NZ)
    vmem = pltpu.VMEM
    dma = pltpu.SemaphoreType.DMA
    return pl.pallas_call(
        kernel,
        out_shape=jax.ShapeDtypeStruct((rows, hidden), BF),
        in_specs=[pl.BlockSpec(memory_space=vmem)] * 3
        + [pl.BlockSpec(memory_space=pl.ANY)] * 5,
        out_specs=pl.BlockSpec(memory_space=vmem),
        scratch_shapes=[
            vmem(self_weight1.shape, BF),
            vmem(neigh_weight1.shape, BF),
            vmem(self_weight2.shape, BF),
            vmem(neigh_weight2.shape, BF),
            vmem((n1 + n2, NZ * rows, chunk), BF),
            vmem((n1 + n2, ncol, block, chunk), BF),
            vmem((n1 + n2, ncol, block, chunk), BF),
            vmem((slots, NZ * rows), BF),
            vmem((rows, slots), jnp.int32),
            vmem((rows, slots), BF),
            vmem((rows, slots), BF),
            vmem((rows, LANES), F32),
            vmem((rows, LANES), F32),
            vmem((rows, LANES), F32),
            vmem((rows, LANES), F32),
            vmem((rows, degree), jnp.int32),
            vmem((rows, degree), jnp.int32),
            vmem((rows, degree), jnp.int32),
            vmem((slots // LANES, 1, LANES), jnp.int32),
            vmem((ncol, window, 1, LANES), jnp.int32),
            vmem((rows, hidden), F32),
            vmem((rows, hidden), BF),
            vmem((NX, NZ * rank2, hidden + LANES), BF),
            vmem((NX, NZ * rank2, hidden + LANES), BF),
            vmem((NZ, NX * rank2, hidden + LANES), BF),
            vmem((NZ, NX * rank2, hidden + LANES), BF),
            dma((n1 + 4,)),
            dma((n1 + n2, 2, half)),
            dma((n1 + n2, 2, half)),
            dma,
            dma,
            dma((n1 + n2,)),
            dma((n1 + n2,)),
            dma,
            dma,
            dma,
            dma,
        ],
        compiler_params=pltpu.CompilerParams(
            collective_id=0, has_side_effects=True, vmem_limit_bytes=56 * 2**20
        ),
    )(
        neighbours,
        neighbour_mask,
        layer2_position.reshape(1, rows),
        features,
        self_weight1,
        neigh_weight1,
        self_weight2,
        neigh_weight2,
    )


def solution(mesh):
    spread = P(("grp", "dev"), None)
    return jax.shard_map(
        body,
        mesh=mesh,
        in_specs=(spread, spread, spread, P(("grp", "dev")), P(), P(), P(), P()),
        out_specs=spread,
        check_vma=False,
    )
```

time: 463 us -> 163 us (0.35); the launches traced: 454 us -> 162 us
  Pallas kernels: 0 us -> 158 us
  local copies, waits for them, and re-layouts: 136 us -> 4.55 us
  blocking collectives: 104 us -> 0 us
  waiting for transfers between devices: 104 us -> 0 us
  other arithmetic: 70.3 us -> 0 us
  starting transfers between devices: 29.3 us -> 0 us
  matrix products: 9.57 us -> 0 us
    pallas_call x0 -> x1, Pallas kernels: none -> 158 us  [body(): pl.pallas_call(kernel, out_shape=jax.ShapeDtypeStruct((rows, hidden), BF)...]
    all_to_all x4 -> x0, blocking collectives: 104 us -> none  [the longest x1 39.9 us: body(): lax.all_to_all(reply_second, 'grp', split_axis=0, concat_axis=0, tiled=True)]
    all_to_all x4 -> x0, waiting for transfers between devices: 104 us -> none  [the longest x1 63.2 us: body(): lax.all_to_all(lax.all_to_all(reply_second, 'grp', split_axis=0, concat_a...]
    gather x8 -> x0, local copies, waits for them, and re-layouts: 61.3 us -> none  [the longest x4 22.7 us: serve_rows(): picked = source[asked_rows]]
    scatter x6 -> x0, local copies, waits for them, and re-layouts: 37.2 us -> none  [the longest x2 16.8 us: slot_of(): ranks = jnp.zeros((item_count,), jnp.int32).at[ordering].set(ranked)]
    all_to_all x4 -> x0, starting transfers between devices: 29.3 us -> none  [the longest x1 10.3 us: body(): lax.all_to_all(outgoing, 'dev', split_axis=0, concat_axis=0, tiled=True)]
    unnamed x4 -> x0, other arithmetic: 29.3 us -> none
    scatter-add x2 -> x0, other arithmetic: 24.7 us -> none  [slot_of(): per_owner = jnp.zeros((peer_count + 1,), jnp.int32).at[sort_key].add(1)]
  transfers between devices with their start and end apart: 4 -> 0, of which waited for: 3 -> 0; matrix products, arithmetic and copies ran while one was open for 13% -> 0% of each run, Pallas kernels for 0% -> 0%
where the time goes in v1:
time: 163 us; the launch traced here: 162 us
  Pallas kernels  158 us (97%)
  local copies, waits for them, and re-layouts  4.55 us (3%)
    pallas_call x1, Pallas kernels, body(): pl.pallas_call(kernel, out_shape=jax.ShapeDtypeStruct((rows, hidden), BF)...  158 us
    unnamed x3, local copies, waits for them, and re-layouts  4.55 us

profile of v1, /device:TPU:1, one launch (start us, length us, event | category | flops | bytes accessed | tf_op | source)
XLA Modules:
  0.0 162.4 jit_solution(11127845618018554969)
XLA Ops:
  0.0 1.4 copy.9.nb_ref
  1.4 1.4 copy.10.mk_ref
  2.9 157.8 %shard_map.82 = bf16[128,1024]{1,0:T(8,128)(2,1)} custom-call(s32[128,25]{1,0:T(8,128)} %copy.9.nb_ref, s32[128,25]{1,0:T(8,128)} %copy.10.mk_ref, s32[1,128]{1,0:T(1,128)} %bitcast.1, bf16[128,768]{1,0:T(8,128)(2,1)} %feat_hbm.1, bf16[768,1024]{1,0:T(8,128)(2,1)} %ws1_hbm.1, bf16[768,1024]{1,0:T(8,128)(2,1)} %wn1_hbm.1, bf16[1024,1024]{1,0:T(8,128)(2,1)} %ws2_hbm.1, ...), custom_call_target="tpu_custom_call" | custom-call | tf_op jit(solution)/shard_map/pallas_call | solution.py:501
  160.7 1.7 %copy.12 = bf16[128,1024]{1,0:T(8,128)(2,1)} copy(bf16[128,1024]{1,0:T(8,128)(2,1)} %shard_map.82) | data formatting | bytes 524288

commit v2 on v1

v2 whole, which is shorter than its diff:
```python
import jax
import jax.numpy as jnp
from jax import lax
from jax.experimental import pallas as pl
from jax.experimental.pallas import tpu as pltpu
from jax.sharding import PartitionSpec as P

NX, NZ, NC = 4, 8, 2
CAP = 6
LANES = 128
BF = jnp.bfloat16
F32 = jnp.float32
MESH = pl.DeviceIdType.MESH


def iota(shape, dim):
    return lax.broadcasted_iota(jnp.int32, shape, dim)


def mm(a, b):
    return jnp.dot(a, b, preferred_element_type=F32)


def one_zero(cond):
    return jnp.where(cond, 1.0, 0.0).astype(BF)


def spans(first, units):
    cuts = [(first, 1)]
    at = first + 1
    while at < first + units:
        wide = 2 if at + 2 < first + units else 1
        cuts.append((at, wide))
        at += wide
    return cuts


def kernel(
    nb_ref,
    mk_ref,
    pos_ref,
    feat_hbm,
    ws1_hbm,
    wn1_hbm,
    ws2_hbm,
    wn2_hbm,
    out_ref,
    ws1,
    wn1,
    ws2,
    wn2,
    table,
    serve,
    ans,
    pick,
    key_ref,
    adj,
    adj2,
    loc,
    loc2,
    cnt2,
    slots,
    slot_p,
    slot_id,
    slot_row,
    lists,
    asked,
    acc,
    hid,
    pos_out,
    pos_in,
    fold,
    leave,
    land,
    load_sem,
    near_send,
    near_recv,
    ring_send,
    ring_recv,
    req_send,
    req_recv,
    pos_send,
    pos_recv,
    ans_send,
    ans_recv,
    out_send,
    out_recv,
):
    degree, rows = nb_ref.shape
    ny = lax.axis_size("grp")
    n_dev = NX * NZ * NC
    plane = ny * NC
    ncol = NX * plane
    block = CAP * NZ
    n1 = feat_hbm.shape[1] // LANES
    hidden_width = wn2.shape[0]
    n2 = hidden_width // LANES
    half = NZ // 2
    rank2 = rows // (NX * NZ)
    pieces1 = spans(0, n1)
    pieces2 = spans(n1, n2)
    me_y = lax.axis_index("grp")
    me_dev = lax.axis_index("dev")
    me_x = lax.div(me_dev, NZ * NC)
    me_z = lax.rem(lax.div(me_dev, NC), NZ)
    me_c = lax.rem(me_dev, NC)
    at_x = [lax.rem(me_x + k, NX) * (NZ * NC) for k in range(NX)]
    at_y = [lax.rem(me_y + k, ny) for k in range(ny)]
    at_z = [lax.rem(me_z + k, NZ) * NC for k in range(NZ)]
    at_c = [lax.rem(me_c + k, NC) for k in range(NC)]

    def ahead(d):
        return (
            at_y[d // NC % ny],
            at_x[d // plane] + at_z[0] + at_c[d % NC],
        )

    def behind(d):
        return (
            at_y[-(d // NC % ny) % ny],
            at_x[-(d // plane) % NX] + at_z[0] + at_c[-(d % NC) % NC],
        )

    def owner_at(d):
        return (me_y, at_x[d // NZ] + at_z[d % NZ] + me_c)

    def along_z(dz):
        return (me_y, at_x[0] + at_z[dz] + me_c)

    def drain(ref, sem):
        pltpu.make_async_copy(ref, ref, sem).wait()

    def send(src, dst, out, into, device):
        return pltpu.make_async_remote_copy(
            src_ref=src,
            dst_ref=dst,
            send_sem=out,
            recv_sem=into,
            device_id=device,
            device_id_type=MESH,
        )

    own = pl.ds(pl.multiple_of(me_z * rows, rows), rows)

    loads = []
    for u in range(n1):
        loads.append(
            pltpu.make_async_copy(
                feat_hbm.at[:, pl.ds(u * LANES, LANES)],
                table.at[u, own],
                load_sem.at[u],
            )
        )
    for k, (far, near) in enumerate(
        ((ws1_hbm, ws1), (wn1_hbm, wn1), (ws2_hbm, ws2), (wn2_hbm, wn2))
    ):
        loads.append(pltpu.make_async_copy(far, near, load_sem.at[n1 + k]))
    for u in range(n1):
        loads[u].start()

    barrier = pltpu.get_barrier_semaphore()
    peers = [along_z(dz) for dz in range(1, NZ)]
    peers += [ahead(d) for d in range(1, ncol)]
    peers += [owner_at(d) for d in range(1, NX * NZ) if d // NZ and d % NZ]
    for peer in peers:
        pl.semaphore_signal(barrier, inc=1, device_id=peer, device_id_type=MESH)
    for load in loads[n1:]:
        load.start()

    nb = nb_ref[...]
    mk = mk_ref[...]
    owner = nb // rows
    row = nb % rows
    o_y = owner // n_dev
    o_dev = owner % n_dev
    o_x = o_dev // (NZ * NC)
    o_z = o_dev // NC % NZ
    o_c = o_dev % NC
    mine = owner == me_y * n_dev + me_dev
    valid = mk > 0
    remote = valid & jnp.logical_not(mine)
    col = (
        ((me_x + NX - o_x) % NX) * plane
        + ((me_y + ny - o_y) % ny) * NC
        + (me_c + NC - o_c) % NC
    )
    far_col = jnp.where(remote, col, -4096)

    pack = LANES // ncol
    lane = iota((rows, LANES), 1)
    sub = iota((rows, LANES), 0)
    sooner = one_zero(sub < lane)
    ones = jnp.ones((rows, LANES), BF)
    same = lane % ncol == sub % ncol
    every = one_zero(same)
    before = one_zero(same & (lane // ncol < sub // ncol))
    so_far = jnp.zeros((rows, LANES), F32)
    slots[...] = jnp.full_like(slots, -1)
    for j in range(0, degree, pack):
        members = range(j, min(j + pack, degree))
        hot = jnp.zeros((rows, LANES), jnp.bool_)
        for s in members:
            hot = hot | (far_col[s : s + 1, :] == sub - (s - j) * ncol)
        hot = one_zero(hot)
        totals = mm(hot, ones)
        rank = (
            mm(hot, sooner)
            + mm(before, totals.astype(BF))
            + mm(every, so_far.astype(BF))
        )
        so_far = so_far + totals
        rank = rank * hot.astype(F32)
        for s in members:
            part = rank[(s - j) * ncol : (s - j + 1) * ncol, :]
            slots[0, s : s + 1, :] = jnp.sum(part, axis=0, keepdims=True).astype(jnp.int32)
    slots[0, 0:degree, :] = jnp.where(remote, col * block + slots[0, 0:degree, :], -1)
    slots[1, 0:degree, :] = o_z * rows + row + 1
    slots[2, 0:degree, :] = jnp.where(valid & mine, row, -1)
    slot_p[...] = slots[0].T
    slot_id[...] = slots[1].T
    slot_row[...] = slots[2].T
    count = jnp.sum(mk.astype(F32), axis=0, keepdims=True)
    diagonal = jnp.where(sub == lane, count, 0.0).astype(BF)
    cnt = mm(diagonal, ones)

    for u in range(n1):
        loads[u].wait()
    pl.semaphore_wait(barrier, len(peers))

    def wide_at(piece, z, start, size):
        first, wide = piece
        return table.at[
            pl.ds(first, wide), pl.ds(pl.multiple_of(z * rows + start, rows // 2), size)
        ]

    def near_all(layer, piece):
        mine_at = wide_at(piece, me_z, 0, rows)
        for dz in (4, 3, 5, 2, 6, 1, 7):
            send(
                mine_at, mine_at, near_send.at[layer], near_recv.at[layer], along_z(dz)
            ).start()

    def near_wait(layer, piece, sem):
        first, wide = piece
        drain(table.at[pl.ds(first, wide), pl.ds(0, (NZ - 1) * rows)], sem.at[layer])

    def ring_block(piece, s, way, last):
        back = -(s - 1) % NZ if way == 0 else (s - 1) % NZ
        z = lax.rem(me_z + back, NZ)
        if last:
            return wide_at(piece, z, way * (rows // 2), rows // 2)
        return wide_at(piece, z, 0, rows)

    def ring_op(piece, s):
        for way in range(2):
            if s > 1:
                drain(
                    ring_block(piece, s, way, False), ring_recv.at[piece[0], way, s - 2]
                )
            if s <= half:
                ref = ring_block(piece, s, way, s == half)
                send(
                    ref,
                    ref,
                    ring_send.at[piece[0], way, s - 1],
                    ring_recv.at[piece[0], way, s - 1],
                    along_z(1 if way == 0 else NZ - 1),
                ).start()

    def ring_end(piece):
        for way in range(2):
            drain(
                ring_block(piece, half + 1, way, True),
                ring_recv.at[piece[0], way, half - 1],
            )

    def turn(pieces, t):
        for p in range(1, len(pieces)):
            if 1 <= t - (p - 1) <= half:
                ring_op(pieces[p], t - (p - 1))

    near_all(0, pieces1[0])
    turn(pieces1, 1)

    tiles = ncol * block // LANES
    lists[...] = jnp.zeros_like(lists)

    @pl.loop(0, rows // 8)
    def _(i):
        at_rows = pl.ds(pl.multiple_of(i * 8, 8), 8)
        p8 = slot_p[at_rows, :]
        id8 = slot_id[at_rows, :]
        row8 = slot_row[at_rows, :]
        lane8 = iota((8, LANES), 1)
        p_all = [jnp.broadcast_to(p8[:, s : s + 1], (8, LANES)) for s in range(degree)]
        id_all = [jnp.broadcast_to(id8[:, s : s + 1], (8, LANES)) for s in range(degree)]
        for t in range(tiles):
            got = jnp.zeros((8, LANES), jnp.int32)
            for s in range(degree):
                got = jnp.where(p_all[s] == lane8 + t * LANES, id_all[s], got)
            key_ref[at_rows, t * LANES : (t + 1) * LANES] = got
            lists[t] = lists[t] + jnp.sum(got, axis=0, keepdims=True)
        near = jnp.zeros((8, LANES), F32)
        for s in range(degree):
            near = near + jnp.where(row8[:, s : s + 1] == lane8, 1.0, 0.0)
        loc[at_rows, :] = near

    window = 8 * block // LANES
    for d in range(1, ncol):
        send(
            lists.at[pl.ds(d // 8 * window, window)],
            asked.at[d],
            req_send,
            req_recv,
            behind(d),
        ).start()
    asked[0] = lists[0:window]
    turn(pieces1, 2)

    pos = pos_ref[...]
    t_dev = pos // rows % n_dev
    t_x = t_dev // (NZ * NC)
    t_z = t_dev // NC % NZ
    target = ((t_x + NX - me_x) % NX) * NZ + (t_z + NZ - me_z) % NZ
    hot_t = iota((NX * NZ, rows), 0) == target
    ahead_of = mm(one_zero(hot_t), sooner)
    rank_t = jnp.sum(jnp.where(hot_t, ahead_of, 0.0), axis=0, keepdims=True)
    move = one_zero(target * rank2 + rank_t.astype(jnp.int32) == sub)
    pos_8 = jnp.broadcast_to((pos % rows).astype(F32), (16, rows)).astype(BF)
    pos_t = lax.dot_general(
        pos_8, move, (((1,), (1,)), ((), ())), preferred_element_type=F32
    )
    pos_out[...] = pos_t[0:8, :]
    for d in range(1, NX * NZ):
        send(pos_out, pos_in.at[d], pos_send, pos_recv, owner_at(d)).start()
    pos_in[0] = pos_out[...]
    adj[...] = one_zero(key_ref[...] > 0)
    adj2[...] = mm(move, adj[...]).astype(BF)
    loc2[...] = mm(move, loc[...].astype(BF))
    cnt2[...] = mm(move, cnt.astype(BF))

    drain(asked.at[pl.ds(1, ncol - 1)], req_recv)
    turn(pieces1, 3)

    @pl.loop(0, ncol)
    def _(d):
        got = asked[d]
        spot = iota((block, LANES), 0) + lax.rem(d, 8) * block
        found = jnp.zeros((block, LANES), jnp.int32)
        for t in range(window):
            piece = jnp.broadcast_to(got[t], (block, LANES))
            found = found + jnp.where(iota((block, LANES), 1) + t * LANES == spot, piece, 0)
        found = jnp.sum(found, axis=1, keepdims=True)
        hit = iota((block, NZ * rows), 1) + 1 == found
        pick[pl.ds(pl.multiple_of(d * block, block), block), :] = one_zero(hit)

    def joined(ref, piece, *index):
        first, wide = piece
        return jnp.concatenate([ref[(u, *index)] for u in range(first, first + wide)], 1)

    def serve_piece(piece):
        first, wide = piece

        @pl.loop(0, NX)
        def _(j):
            some = pl.ds(pl.multiple_of(j * plane * block, plane * block), plane * block)
            picked = mm(pick[some, :], joined(table, piece)).astype(BF)
            picked = picked.reshape(plane, block, wide * LANES)
            for k in range(wide):
                serve[first + k, pl.ds(j * plane, plane)] = picked[
                    :, :, k * LANES : (k + 1) * LANES
                ]
            base = lax.rem(me_x + j, NX) * (NZ * NC) + at_z[0]
            for i in range(plane):
                cp = send(
                    serve.at[pl.ds(first, wide), j * plane + i],
                    ans.at[pl.ds(first, wide), j * plane + i],
                    ans_send.at[first],
                    ans_recv.at[first],
                    (at_y[i // NC], base + at_c[i % NC]),
                )
                if i == 0:
                    pl.when(j > 0)(cp.start)
                else:
                    cp.start()

        for k in range(wide):
            ans[first + k, 0] = serve[first + k, 0]

    def serve_layer(layer, pieces):
        near_wait(layer, pieces[0], near_recv)
        serve_piece(pieces[0])
        turn(pieces, half)
        for p in range(1, len(pieces)):
            ring_end(pieces[p])
            serve_piece(pieces[p])
            turn(pieces, half + p)

    def answers(piece, ref):
        return ref.at[pl.ds(piece[0], piece[1]), pl.ds(1, ncol - 1)]

    def mean(piece, adjacency, near, degrees):
        first, wide = piece
        drain(answers(piece, ans), ans_recv.at[first])
        rows_in = jnp.concatenate(
            [ans[first + k].reshape(ncol * block, LANES) for k in range(wide)], 1
        )
        summed = mm(adjacency[...], rows_in) + mm(near, joined(table, piece, own))
        return (summed / degrees).astype(BF)

    def cut(piece, start=0):
        return slice((piece[0] - start) * LANES, (piece[0] - start + piece[1]) * LANES)

    serve_layer(0, pieces1)
    loads[n1].wait()
    loads[n1 + 1].wait()
    x = jnp.concatenate([table[u, own, :] for u in range(n1)], 1)
    for q in pieces2:
        acc[:, cut(q, n1)] = mm(x, ws1[:, cut(q, n1)])
    near1 = loc[...].astype(BF)
    degrees1 = cnt[:, 0:1]
    for q in pieces1[:-1]:
        acc[...] += mm(mean(q, adj, near1, degrees1), wn1[cut(q), :])
    m = mean(pieces1[-1], adj, near1, degrees1)
    for i, q in enumerate(pieces2):
        total = acc[:, cut(q, n1)] + mm(m, wn1[cut(pieces1[-1]), cut(q, n1)])
        total = jnp.maximum(total, 0.0).astype(BF)
        for k in range(q[1]):
            table[q[0] + k, own, :] = total[:, k * LANES : (k + 1) * LANES]
        if i == 0:
            near_all(1, q)
        if i == 1:
            turn(pieces2, 1)
    turn(pieces2, 2)
    hid[...] = mm(
        move, jnp.concatenate([table[n1 + u, own, :] for u in range(n2)], 1)
    ).astype(BF)
    turn(pieces2, 3)
    serve_layer(1, pieces2)
    loads[n1 + 2].wait()
    loads[n1 + 3].wait()
    for q in pieces2:
        acc[:, cut(q, n1)] = mm(hid[...], ws2[:, cut(q, n1)])
    drain(pos_in.at[pl.ds(1, NX * NZ - 1)], pos_recv)
    near2 = loc2[...].astype(BF)
    for q in pieces2:
        acc[...] += mm(mean(q, adj2, near2, cnt2[:, 0:1]), wn2[cut(q, n1), :])

    fold_rows = 2 * rank2
    pairs = NX * NZ // 2
    low = sub % fold_rows < rank2
    for t in range(n2 // 2):
        a = acc[:, 2 * t * LANES : (2 * t + 1) * LANES]
        b = acc[:, (2 * t + 1) * LANES : (2 * t + 2) * LANES]
        inner = slice(t * fold_rows, (t + 1) * fold_rows)
        first = jnp.where(low, a, pltpu.roll(b, rank2, 0))
        second = jnp.where(low, pltpu.roll(a, rows - rank2, 0), b)
        fold[0:pairs, inner, :] = first.reshape(pairs, fold_rows, LANES)
        fold[pairs:, inner, :] = second.reshape(pairs, fold_rows, LANES)
    leave[...] = fold[...].astype(BF)
    for d in range(1, NX * NZ):
        send(
            leave.at[d % 2 * pairs + d // 2],
            land.at[d % 2 * pairs + d // 2],
            out_send,
            out_recv,
            owner_at(d),
        ).start()
    land[0] = leave[0]

    here = jnp.zeros((1, LANES), F32)
    for d in range(NX * NZ):
        mine_d = iota((1, LANES), 1) // rank2 == d
        here = jnp.where(mine_d, pos_in[d, 0:1, :], here)
    put = one_zero(here == sub.astype(F32))

    drain(land.at[pl.ds(1, 2 * pairs - 1)], out_recv)
    fold[...] = land[...].astype(F32)
    for t in range(n2 // 2):
        inner = slice(t * fold_rows, (t + 1) * fold_rows)
        first = fold[0:pairs, inner, :].reshape(rows, LANES)
        second = fold[pairs:, inner, :].reshape(rows, LANES)
        a = jnp.where(low, first, pltpu.roll(second, rank2, 0))
        b = jnp.where(low, pltpu.roll(first, rows - rank2, 0), second)
        both = jnp.concatenate([a, b], 1).astype(BF)
        out_ref[:, 2 * t * LANES : (2 * t + 2) * LANES] = mm(put, both).astype(BF)

    drain(asked.at[pl.ds(1, ncol - 1)], req_send)
    drain(pos_in.at[pl.ds(1, NX * NZ - 1)], pos_send)
    drain(leave.at[pl.ds(1, 2 * pairs - 1)], out_send)
    for layer, pieces in enumerate((pieces1, pieces2)):
        near_wait(layer, pieces[0], near_send)
        for q in pieces:
            drain(answers(q, serve), ans_send.at[q[0]])
        for q in pieces[1:]:
            for way in range(2):
                for s in range(1, half + 1):
                    drain(
                        ring_block(q, s, way, s == half), ring_send.at[q[0], way, s - 1]
                    )


def body(
    features,
    neighbours,
    neighbour_mask,
    layer2_position,
    self_weight1,
    neigh_weight1,
    self_weight2,
    neigh_weight2,
):
    rows, width = features.shape
    hidden = self_weight1.shape[1]
    ny = lax.axis_size("grp")
    ncol = NX * ny * NC
    block = CAP * NZ
    slots = ncol * block
    units = (width + hidden) // LANES
    half = NZ // 2
    window = 8 * block // LANES
    rank2 = rows // (NX * NZ)
    deep = hidden // LANES * rank2
    vmem = pltpu.VMEM
    dma = pltpu.SemaphoreType.DMA
    return pl.pallas_call(
        kernel,
        out_shape=jax.ShapeDtypeStruct((rows, hidden), BF),
        in_specs=[pl.BlockSpec(memory_space=vmem)] * 3
        + [pl.BlockSpec(memory_space=pl.ANY)] * 5,
        out_specs=pl.BlockSpec(memory_space=vmem),
        scratch_shapes=[
            vmem(self_weight1.shape, BF),
            vmem(neigh_weight1.shape, BF),
            vmem(self_weight2.shape, BF),
            vmem(neigh_weight2.shape, BF),
            vmem((units, NZ * rows, LANES), BF),
            vmem((units, ncol, block, LANES), BF),
            vmem((units, ncol, block, LANES), BF),
            vmem((slots, NZ * rows), BF),
            vmem((rows, slots), jnp.int32),
            vmem((rows, slots), BF),
            vmem((rows, slots), BF),
            vmem((rows, LANES), F32),
            vmem((rows, LANES), F32),
            vmem((rows, LANES), F32),
            vmem((3, 32, rows), jnp.int32),
            vmem((rows, 32), jnp.int32),
            vmem((rows, 32), jnp.int32),
            vmem((rows, 32), jnp.int32),
            vmem((slots // LANES, 1, LANES), jnp.int32),
            vmem((ncol, window, 1, LANES), jnp.int32),
            vmem((rows, hidden), F32),
            vmem((rows, hidden), BF),
            vmem((8, LANES), F32),
            vmem((NX * NZ, 8, LANES), F32),
            vmem((NX * NZ, deep, LANES), F32),
            vmem((NX * NZ, deep, LANES), BF),
            vmem((NX * NZ, deep, LANES), BF),
            dma((width // LANES + 4,)),
            dma((2,)),
            dma((2,)),
            dma((units, 2, half)),
            dma((units, 2, half)),
            dma,
            dma,
            dma,
            dma,
            dma((units,)),
            dma((units,)),
            dma,
            dma,
        ],
        compiler_params=pltpu.CompilerParams(
            collective_id=0, has_side_effects=True, vmem_limit_bytes=56 * 2**20
        ),
    )(
        neighbours.T,
        neighbour_mask.T,
        layer2_position.reshape(1, rows),
        features,
        self_weight1,
        neigh_weight1,
        self_weight2,
        neigh_weight2,
    )


def solution(mesh):
    spread = P(("grp", "dev"), None)
    return jax.shard_map(
        body,
        mesh=mesh,
        in_specs=(spread, spread, spread, P(("grp", "dev")), P(), P(), P(), P()),
        out_specs=spread,
        check_vma=False,
    )
```

time: 163 us -> 128 us (0.79)
  Pallas kernels: 158 us -> 126 us
  local copies, waits for them, and re-layouts: 4.55 us -> 1.67 us
    pallas_call x1, Pallas kernels: 158 us -> 126 us  [body(): pl.pallas_call(kernel, out_shape=jax.ShapeDtypeStruct((rows, hidden), BF)...]
    unnamed x3 -> x1, local copies, waits for them, and re-layouts: 4.55 us -> 1.67 us
where the time goes in v2:
time: 128 us
  Pallas kernels  126 us (98%)
  local copies, waits for them, and re-layouts  1.67 us (1%)
    pallas_call x1, Pallas kernels, body(): pl.pallas_call(kernel, out_shape=jax.ShapeDtypeStruct((rows, hidden), BF)...  126 us

profile of v2, /device:TPU:1, one launch (start us, length us, event | category | flops | bytes accessed | tf_op | source)
XLA Modules:
  0.0 128.0 jit_solution(11649998394526774721)
XLA Ops:
  0.0 126.4 %shard_map.82 = bf16[128,1024]{1,0:T(8,128)(2,1)} custom-call(s32[25,128]{1,0:T(8,128)} %bitcast.3, s32[25,128]{1,0:T(8,128)} %bitcast.4, s32[1,128]{1,0:T(1,128)} %bitcast.5, bf16[128,768]{1,0:T(8,128)(2,1)} %feat_hbm.1, bf16[768,1024]{1,0:T(8,128)(2,1)} %ws1_hbm.1, bf16[768,1024]{1,0:T(8,128)(2,1)} %wn1_hbm.1, bf16[1024,1024]{1,0:T(8,128)(2,1)} %ws2_hbm.1, ...), custom_call_target="tpu_custom_call" | custom-call | tf_op jit(solution)/shard_map/pallas_call | solution.py:526
  126.4 1.7 %copy.10 = bf16[128,1024]{1,0:T(8,128)(2,1)} copy(bf16[128,1024]{1,0:T(8,128)(2,1)} %shard_map.82) | data formatting | bytes 524288

commit v3 on v2

v3 whole, which is shorter than its diff:
```python
import jax
import jax.numpy as jnp
from jax import lax
from jax.experimental import pallas as pl
from jax.experimental.pallas import tpu as pltpu
from jax.sharding import PartitionSpec as P

NX, NZ, NC = 4, 8, 2
CAP = 6
LANES = 128
BF = jnp.bfloat16
F32 = jnp.float32
MESH = pl.DeviceIdType.MESH


def iota(shape, dim):
    return lax.broadcasted_iota(jnp.int32, shape, dim)


def mm(a, b):
    return jnp.dot(a, b, preferred_element_type=F32)


def one_zero(cond):
    return jnp.where(cond, 1.0, 0.0).astype(BF)


PLACES = (1, NZ - 1, 0, 2, NZ - 2, 3, NZ - 3, 4)
OWN = PLACES.index(0)
ROW = 16


def place_of(dz):
    return PLACES.index(dz % NZ)


def kernel(
    nb_ref,
    mk_ref,
    pos_ref,
    feat_hbm,
    ws1_hbm,
    wn1_hbm,
    ws2_hbm,
    wn2_hbm,
    out_ref,
    ws1,
    wn1,
    ws2,
    wn2,
    table1,
    table2,
    serve1,
    serve2,
    ans1,
    ans2,
    pick,
    key_ref,
    adj,
    adj2,
    loc,
    loc2,
    cnt2,
    slots,
    slot_p,
    slot_id,
    slot_row,
    lists,
    asked,
    acc,
    hid,
    pos_out,
    pos_in,
    fold,
    leave,
    land,
    load_sem,
    ring_send,
    ring_recv,
    req_send,
    req_recv,
    pos_send,
    pos_recv,
    ans_send,
    ans_recv,
    out_send,
    out_recv,
):
    degree, rows = nb_ref.shape
    ny = lax.axis_size("grp")
    n_dev = NX * NZ * NC
    plane = ny * NC
    ncol = NX * plane
    block = CAP * NZ
    blocks = block // ROW
    per_block = ncol * ROW
    hidden_width = wn2.shape[0]
    n2 = hidden_width // LANES
    half = NZ // 2
    rank2 = rows // (NX * NZ)
    me_y = lax.axis_index("grp")
    me_dev = lax.axis_index("dev")
    me_x = lax.div(me_dev, NZ * NC)
    me_z = lax.rem(lax.div(me_dev, NC), NZ)
    me_c = lax.rem(me_dev, NC)
    at_x = [lax.rem(me_x + k, NX) * (NZ * NC) for k in range(NX)]
    at_y = [lax.rem(me_y + k, ny) for k in range(ny)]
    at_z = [lax.rem(me_z + k, NZ) * NC for k in range(NZ)]
    at_c = [lax.rem(me_c + k, NC) for k in range(NC)]

    def ahead(d):
        return (
            at_y[d // NC % ny],
            at_x[d // plane] + at_z[0] + at_c[d % NC],
        )

    def behind(d):
        return (
            at_y[-(d // NC % ny) % ny],
            at_x[-(d // plane) % NX] + at_z[0] + at_c[-(d % NC) % NC],
        )

    def owner_at(d):
        return (me_y, at_x[d // NZ] + at_z[d % NZ] + me_c)

    def along_z(dz):
        return (me_y, at_x[0] + at_z[dz] + me_c)

    def drain(ref, sem):
        pltpu.make_async_copy(ref, ref, sem).wait()

    def send(src, dst, out, into, device):
        return pltpu.make_async_remote_copy(
            src_ref=src,
            dst_ref=dst,
            send_sem=out,
            recv_sem=into,
            device_id=device,
            device_id_type=MESH,
        )

    own = slice(OWN * rows, (OWN + 1) * rows)

    loads = [
        pltpu.make_async_copy(far, near, load_sem.at[k])
        for k, (far, near) in enumerate(
            (
                (feat_hbm, table1.at[pl.ds(OWN * rows, rows)]),
                (ws1_hbm, ws1),
                (wn1_hbm, wn1),
                (ws2_hbm, ws2),
                (wn2_hbm, wn2),
            )
        )
    ]
    loads[0].start()

    barrier = pltpu.get_barrier_semaphore()
    peers = [along_z(dz) for dz in range(1, NZ)]
    peers += [ahead(d) for d in range(1, ncol)]
    peers += [owner_at(d) for d in range(1, NX * NZ) if d // NZ and d % NZ]
    for peer in peers:
        pl.semaphore_signal(barrier, inc=1, device_id=peer, device_id_type=MESH)
    for load in loads[1:]:
        load.start()

    nb = nb_ref[...]
    mk = mk_ref[...]
    owner = nb // rows
    row = nb % rows
    o_y = owner // n_dev
    o_dev = owner % n_dev
    o_x = o_dev // (NZ * NC)
    o_z = o_dev // NC % NZ
    o_c = o_dev % NC
    mine = owner == me_y * n_dev + me_dev
    valid = mk > 0
    remote = valid & jnp.logical_not(mine)
    col = (
        ((me_x + NX - o_x) % NX) * plane
        + ((me_y + ny - o_y) % ny) * NC
        + (me_c + NC - o_c) % NC
    )
    away = (o_z + NZ - me_z) % NZ
    nearness = jnp.zeros_like(away)
    for k, dz in enumerate(PLACES):
        nearness = jnp.where(away == dz, k, nearness)

    lane = iota((rows, LANES), 1)
    sub = iota((rows, LANES), 0)
    sooner = one_zero(sub < lane)
    ones = jnp.ones((rows, LANES), BF)
    sooner_all = jnp.concatenate([sooner, ones], 1)
    slots[...] = jnp.full_like(slots, -1)
    slots[3, 0:degree, :] = jnp.where(remote, nearness * ncol + col, -1)

    def rank_slot(s, so_far):
        hot = slots[3, pl.ds(s, 1), :] == iota((NZ * ncol, rows), 0)
        counted = mm(one_zero(hot), sooner_all)
        rank = jnp.where(hot, counted[:, :rows] + so_far, 0.0)
        slots[0, pl.ds(s, 1), :] = jnp.sum(rank, axis=0, keepdims=True).astype(jnp.int32)
        return so_far + counted[:, rows:]

    lax.fori_loop(0, degree, rank_slot, jnp.zeros((NZ * ncol, rows), F32))
    spot = nearness * CAP + slots[0, 0:degree, :]
    slots[0, 0:degree, :] = jnp.where(
        remote, spot // ROW * per_block + col * ROW + spot % ROW, -1
    )
    slots[1, 0:degree, :] = nearness * rows + row + 1
    slots[2, 0:degree, :] = jnp.where(valid & mine, row, -1)
    slot_p[...] = slots[0].T
    slot_id[...] = slots[1].T
    slot_row[...] = slots[2].T
    count = jnp.sum(mk.astype(F32), axis=0, keepdims=True)
    diagonal = jnp.where(sub == lane, count, 0.0).astype(BF)
    cnt = mm(diagonal, ones)

    loads[0].wait()
    pl.semaphore_wait(barrier, len(peers))

    def part_of(table, dz, h):
        wide = table.shape[1] // 2
        return table.at[pl.ds(place_of(dz) * rows, rows), pl.ds(h * wide, wide)]

    def moves(s):
        for way, sign in enumerate((-1, 1)):
            for h in range(2):
                if s < half or h == way:
                    yield way, sign, h

    def ring_start(layer, table, s, halves=(0, 1)):
        for way, sign, h in moves(s):
            if h in halves:
                send(
                    part_of(table, sign * (s - 1), h),
                    part_of(table, sign * s, h),
                    ring_send.at[layer, way, s - 1, h],
                    ring_recv.at[layer, way, s - 1, h],
                    along_z(1 if way == 0 else NZ - 1),
                ).start()

    def ring_wait(layer, table, s, halves=(0, 1)):
        for way, sign, h in moves(s):
            if h in halves:
                drain(part_of(table, sign * s, h), ring_recv.at[layer, way, s - 1, h])

    def ring_left(layer, table):
        for s in range(1, half + 1):
            for way, sign, h in moves(s):
                drain(
                    part_of(table, sign * (s - 1), h), ring_send.at[layer, way, s - 1, h]
                )

    ring_start(0, table1, 1)

    tiles = ncol * block // LANES
    lists[...] = jnp.zeros_like(lists)

    @pl.loop(0, rows // 8)
    def _(i):
        at_rows = pl.ds(pl.multiple_of(i * 8, 8), 8)
        p8 = slot_p[at_rows, :]
        id8 = slot_id[at_rows, :]
        row8 = slot_row[at_rows, :]
        lane8 = iota((8, LANES), 1)
        p_all = [jnp.broadcast_to(p8[:, s : s + 1], (8, LANES)) for s in range(degree)]
        id_all = [jnp.broadcast_to(id8[:, s : s + 1], (8, LANES)) for s in range(degree)]
        for t in range(tiles):
            got = jnp.zeros((8, LANES), jnp.int32)
            for s in range(degree):
                got = jnp.where(p_all[s] == lane8 + t * LANES, id_all[s], got)
            key_ref[at_rows, t * LANES : (t + 1) * LANES] = got
            at_list = t % (tiles // blocks) * blocks + t // (tiles // blocks)
            lists[at_list] = lists[at_list] + jnp.sum(got, axis=0, keepdims=True)
        near = jnp.zeros((8, LANES), F32)
        for s in range(degree):
            near = near + jnp.where(row8[:, s : s + 1] == lane8, 1.0, 0.0)
        loc[at_rows, :] = near

    window = blocks
    for d in range(1, ncol):
        send(
            lists.at[pl.ds(d // 8 * window, window)],
            asked.at[d],
            req_send,
            req_recv,
            behind(d),
        ).start()
    asked[0] = lists[0:window]
    ring_wait(0, table1, 1, (0,))
    ring_start(0, table1, 2, (0,))

    pos = pos_ref[...]
    t_dev = pos // rows % n_dev
    t_x = t_dev // (NZ * NC)
    t_z = t_dev // NC % NZ
    target = ((t_x + NX - me_x) % NX) * NZ + (t_z + NZ - me_z) % NZ
    hot_t = iota((NX * NZ, rows), 0) == target
    ahead_of = mm(one_zero(hot_t), sooner)
    rank_t = jnp.sum(jnp.where(hot_t, ahead_of, 0.0), axis=0, keepdims=True)
    move = one_zero(target * rank2 + rank_t.astype(jnp.int32) == sub)
    pos_8 = jnp.broadcast_to((pos % rows).astype(F32), (16, rows)).astype(BF)
    pos_t = lax.dot_general(
        pos_8, move, (((1,), (1,)), ((), ())), preferred_element_type=F32
    )
    pos_out[...] = pos_t[0:8, :]
    for d in range(1, NX * NZ):
        send(pos_out, pos_in.at[d], pos_send, pos_recv, owner_at(d)).start()
    pos_in[0] = pos_out[...]
    adj[...] = one_zero(key_ref[...] > 0)
    adj2[...] = mm(move, adj[...]).astype(BF)
    loc2[...] = mm(move, loc[...].astype(BF))
    cnt2[...] = mm(move, cnt.astype(BF))

    drain(asked.at[pl.ds(1, ncol - 1)], req_recv)

    reach = []
    for b in range(blocks):
        first, last = b * ROW // CAP, ((b + 1) * ROW - 1) // CAP
        reach.append((first * rows, (last + 1 - first) * rows))

    @pl.loop(0, ncol)
    def _(d):
        got = asked[d]
        spot = iota((ROW, LANES), 0) + lax.rem(d, 8) * ROW
        for b in range(blocks):
            first, deep = reach[b]
            piece = jnp.broadcast_to(got[b], (ROW, LANES))
            found = jnp.where(iota((ROW, LANES), 1) == spot, piece, 0)
            found = jnp.sum(found, axis=1, keepdims=True)
            hit = iota((ROW, deep), 1) + (first + 1) == found
            some = pl.ds(pl.multiple_of(d * ROW, ROW), ROW)
            pick[b, some, 0:deep] = one_zero(hit)

    def serve_block(layer, table, serve, b, halves):
        first, deep = reach[b]
        wide = table.shape[1] // 2
        at_col, n_col = halves[0] * wide, len(halves) * wide

        @pl.loop(0, NX)
        def _(j):
            some = pl.ds(pl.multiple_of(j * plane * ROW, plane * ROW), plane * ROW)
            picked = mm(
                pick[b, some, 0:deep],
                table[first : first + deep, at_col : at_col + n_col],
            ).astype(BF)
            serve[b, pl.ds(j * plane, plane), :, at_col : at_col + n_col] = picked.reshape(
                plane, ROW, n_col
            )
            base = lax.rem(me_x + j, NX) * (NZ * NC) + at_z[0]
            for i in range(plane):
                cp = send(
                    serve.at[b, j * plane + i, :, pl.ds(at_col, n_col)],
                    (ans1, ans2)[layer].at[b, j * plane + i, :, pl.ds(at_col, n_col)],
                    ans_send.at[layer, b, halves[0]],
                    ans_recv.at[layer, b, halves[0]],
                    (at_y[i // NC], base + at_c[i % NC]),
                )
                if i == 0:
                    pl.when(j > 0)(cp.start)
                else:
                    cp.start()

    def serve_layer(layer, table, serve, ans):
        serve_block(layer, table, serve, 0, (0,))
        ring_wait(layer, table, 1, (1,))
        ring_start(layer, table, 2, (1,))
        serve_block(layer, table, serve, 0, (1,))
        ring_wait(layer, table, 2)
        ring_start(layer, table, 3)
        ring_wait(layer, table, 3)
        ring_start(layer, table, 4)
        serve_block(layer, table, serve, 1, (0, 1))
        ring_wait(layer, table, 4)
        serve_block(layer, table, serve, 2, (0, 1))
        for b in range(blocks):
            ans[b, 0] = serve[b, 0]

    def answers(ref, b, halves):
        wide = ref.shape[3] // 2
        return ref.at[
            b, pl.ds(1, ncol - 1), :, pl.ds(halves[0] * wide, len(halves) * wide)
        ]

    parts = ((0, (0,)), (0, (1,)), (1, (0, 1)), (2, (0, 1)))

    def summed(layer, ans, b, adjacency):
        for part in parts:
            if part[0] == b:
                drain(answers(ans, *part), ans_recv.at[layer, b, part[1][0]])
        return mm(
            adjacency[:, b * per_block : (b + 1) * per_block],
            ans[b].reshape(per_block, ans.shape[3]),
        )

    serve_layer(0, table1, serve1, ans1)
    loads[1].wait()
    loads[2].wait()
    x = table1[own, :]
    acc[...] = mm(x, ws1[...])
    total = mm(loc[...].astype(BF), x)
    for b in range(blocks):
        total = total + summed(0, ans1, b, adj)
    m = (total / cnt[:, 0:1]).astype(BF)
    wide = hidden_width // 2
    for h in range(2):
        cols = slice(h * wide, (h + 1) * wide)
        total = acc[:, cols] + mm(m, wn1[:, cols])
        table2[own, cols] = jnp.maximum(total, 0.0).astype(BF)
        ring_start(1, table2, 1, (h,))
    hid[...] = mm(move, table2[own, :]).astype(BF)
    ring_wait(1, table2, 1, (0,))
    ring_start(1, table2, 2, (0,))
    serve_layer(1, table2, serve2, ans2)
    loads[3].wait()
    loads[4].wait()
    acc[...] = mm(hid[...], ws2[...])
    drain(pos_in.at[pl.ds(1, NX * NZ - 1)], pos_recv)
    total = mm(loc2[...].astype(BF), table2[own, :])
    for b in range(blocks):
        total = total + summed(1, ans2, b, adj2)
    m = (total / cnt2[:, 0:1]).astype(BF)
    acc[...] += mm(m, wn2[...])

    fold_rows = 2 * rank2
    pairs = NX * NZ // 2
    low = sub % fold_rows < rank2
    for t in range(n2 // 2):
        a = acc[:, 2 * t * LANES : (2 * t + 1) * LANES]
        b = acc[:, (2 * t + 1) * LANES : (2 * t + 2) * LANES]
        inner = slice(t * fold_rows, (t + 1) * fold_rows)
        first = jnp.where(low, a, pltpu.roll(b, rank2, 0))
        second = jnp.where(low, pltpu.roll(a, rows - rank2, 0), b)
        fold[0:pairs, inner, :] = first.reshape(pairs, fold_rows, LANES)
        fold[pairs:, inner, :] = second.reshape(pairs, fold_rows, LANES)
    leave[...] = fold[...].astype(BF)
    for d in range(1, NX * NZ):
        send(
            leave.at[d % 2 * pairs + d // 2],
            land.at[d % 2 * pairs + d // 2],
            out_send,
            out_recv,
            owner_at(d),
        ).start()
    land[0] = leave[0]

    here = jnp.zeros((1, LANES), F32)
    for d in range(NX * NZ):
        mine_d = iota((1, LANES), 1) // rank2 == d
        here = jnp.where(mine_d, pos_in[d, 0:1, :], here)
    put = one_zero(here == sub.astype(F32))

    drain(land.at[pl.ds(1, 2 * pairs - 1)], out_recv)
    fold[...] = land[...].astype(F32)
    for t in range(n2 // 2):
        inner = slice(t * fold_rows, (t + 1) * fold_rows)
        first = fold[0:pairs, inner, :].reshape(rows, LANES)
        second = fold[pairs:, inner, :].reshape(rows, LANES)
        a = jnp.where(low, first, pltpu.roll(second, rank2, 0))
        b = jnp.where(low, pltpu.roll(first, rows - rank2, 0), second)
        both = jnp.concatenate([a, b], 1).astype(BF)
        out_ref[:, 2 * t * LANES : (2 * t + 2) * LANES] = mm(put, both).astype(BF)

    drain(asked.at[pl.ds(1, ncol - 1)], req_send)
    drain(pos_in.at[pl.ds(1, NX * NZ - 1)], pos_send)
    drain(leave.at[pl.ds(1, 2 * pairs - 1)], out_send)
    for layer, table, serve in ((0, table1, serve1), (1, table2, serve2)):
        ring_left(layer, table)
        for part in parts:
            drain(answers(serve, *part), ans_send.at[layer, part[0], part[1][0]])


def body(
    features,
    neighbours,
    neighbour_mask,
    layer2_position,
    self_weight1,
    neigh_weight1,
    self_weight2,
    neigh_weight2,
):
    rows, width = features.shape
    hidden = self_weight1.shape[1]
    ny = lax.axis_size("grp")
    ncol = NX * ny * NC
    block = CAP * NZ
    slots = ncol * block
    blocks = block // ROW
    half = NZ // 2
    rank2 = rows // (NX * NZ)
    deep = hidden // LANES * rank2
    vmem = pltpu.VMEM
    dma = pltpu.SemaphoreType.DMA
    return pl.pallas_call(
        kernel,
        out_shape=jax.ShapeDtypeStruct((rows, hidden), BF),
        in_specs=[pl.BlockSpec(memory_space=vmem)] * 3
        + [pl.BlockSpec(memory_space=pl.ANY)] * 5,
        out_specs=pl.BlockSpec(memory_space=vmem),
        scratch_shapes=[
            vmem(self_weight1.shape, BF),
            vmem(neigh_weight1.shape, BF),
            vmem(self_weight2.shape, BF),
            vmem(neigh_weight2.shape, BF),
            vmem((NZ * rows, width), BF),
            vmem((NZ * rows, hidden), BF),
            vmem((blocks, ncol, ROW, width), BF),
            vmem((blocks, ncol, ROW, hidden), BF),
            vmem((blocks, ncol, ROW, width), BF),
            vmem((blocks, ncol, ROW, hidden), BF),
            vmem((blocks, ncol * ROW, 4 * rows), BF),
            vmem((rows, slots), jnp.int32),
            vmem((rows, slots), BF),
            vmem((rows, slots), BF),
            vmem((rows, LANES), F32),
            vmem((rows, LANES), F32),
            vmem((rows, LANES), F32),
            vmem((4, 32, rows), jnp.int32),
            vmem((rows, 32), jnp.int32),
            vmem((rows, 32), jnp.int32),
            vmem((rows, 32), jnp.int32),
            vmem((slots // LANES, 1, LANES), jnp.int32),
            vmem((ncol, blocks, 1, LANES), jnp.int32),
            vmem((rows, hidden), F32),
            vmem((rows, hidden), BF),
            vmem((8, LANES), F32),
            vmem((NX * NZ, 8, LANES), F32),
            vmem((NX * NZ, deep, LANES), F32),
            vmem((NX * NZ, deep, LANES), BF),
            vmem((NX * NZ, deep, LANES), BF),
            dma((5,)),
            dma((2, 2, half, 2)),
            dma((2, 2, half, 2)),
            dma,
            dma,
            dma,
            dma,
            dma((2, blocks, 2)),
            dma((2, blocks, 2)),
            dma,
            dma,
        ],
        compiler_params=pltpu.CompilerParams(
            collective_id=0, has_side_effects=True, vmem_limit_bytes=56 * 2**20
        ),
    )(
        neighbours.T,
        neighbour_mask.T,
        layer2_position.reshape(1, rows),
        features,
        self_weight1,
        neigh_weight1,
        self_weight2,
        neigh_weight2,
    )


def solution(mesh):
    spread = P(("grp", "dev"), None)
    return jax.shard_map(
        body,
        mesh=mesh,
        in_specs=(spread, spread, spread, P(("grp", "dev")), P(), P(), P(), P()),
        out_specs=spread,
        check_vma=False,
    )
```

time: 128 us -> 120 us (0.938)
  Pallas kernels: 126 us -> 118 us
    pallas_call x1, Pallas kernels: 126 us -> 118 us  [body(): pl.pallas_call(kernel, out_shape=jax.ShapeDtypeStruct((rows, hidden), BF)...]
where the time goes in v3:
time: 120 us
  Pallas kernels  118 us (98%)
  local copies, waits for them, and re-layouts  1.67 us (1%)
    pallas_call x1, Pallas kernels, body(): pl.pallas_call(kernel, out_shape=jax.ShapeDtypeStruct((rows, hidden), BF)...  118 us

profile of v3, /device:TPU:1, one launch (start us, length us, event | category | flops | bytes accessed | tf_op | source)
XLA Modules:
  0.0 120.2 jit_solution(16945290027364549644)
XLA Ops:
  0.0 118.5 %shard_map.82 = bf16[128,1024]{1,0:T(8,128)(2,1)} custom-call(s32[25,128]{1,0:T(8,128)} %bitcast.3, s32[25,128]{1,0:T(8,128)} %bitcast.4, s32[1,128]{1,0:T(1,128)} %bitcast.5, bf16[128,768]{1,0:T(8,128)(2,1)} %feat_hbm.1, bf16[768,1024]{1,0:T(8,128)(2,1)} %ws1_hbm.1, bf16[768,1024]{1,0:T(8,128)(2,1)} %wn1_hbm.1, bf16[1024,1024]{1,0:T(8,128)(2,1)} %ws2_hbm.1, ...), custom_call_target="tpu_custom_call" | custom-call | tf_op jit(solution)/shard_map/pallas_call | solution.py:495
  118.5 1.7 %copy.10 = bf16[128,1024]{1,0:T(8,128)(2,1)} copy(bf16[128,1024]{1,0:T(8,128)(2,1)} %shard_map.82) | data formatting | bytes 524288

commit v4 on v3

--- a/solution.py
+++ b/solution.py
@@ -244,6 +244,12 @@
             if h in halves:
                 drain(part_of(table, sign * s, h), ring_recv.at[layer, way, s - 1, h])
 
+    def ring_pass(layer, table, s):
+        for h in range(2):
+            ring_wait(layer, table, s, (h,))
+            if s < half:
+                ring_start(layer, table, s + 1, (h,))
+
     def ring_left(layer, table):
         for s in range(1, half + 1):
             for way, sign, h in moves(s):
@@ -287,30 +293,7 @@
             behind(d),
         ).start()
     asked[0] = lists[0:window]
-    ring_wait(0, table1, 1, (0,))
-    ring_start(0, table1, 2, (0,))
-
-    pos = pos_ref[...]
-    t_dev = pos // rows % n_dev
-    t_x = t_dev // (NZ * NC)
-    t_z = t_dev // NC % NZ
-    target = ((t_x + NX - me_x) % NX) * NZ + (t_z + NZ - me_z) % NZ
-    hot_t = iota((NX * NZ, rows), 0) == target
-    ahead_of = mm(one_zero(hot_t), sooner)
-    rank_t = jnp.sum(jnp.where(hot_t, ahead_of, 0.0), axis=0, keepdims=True)
-    move = one_zero(target * rank2 + rank_t.astype(jnp.int32) == sub)
-    pos_8 = jnp.broadcast_to((pos % rows).astype(F32), (16, rows)).astype(BF)
-    pos_t = lax.dot_general(
-        pos_8, move, (((1,), (1,)), ((), ())), preferred_element_type=F32
-    )
-    pos_out[...] = pos_t[0:8, :]
-    for d in range(1, NX * NZ):
-        send(pos_out, pos_in.at[d], pos_send, pos_recv, owner_at(d)).start()
-    pos_in[0] = pos_out[...]
-    adj[...] = one_zero(key_ref[...] > 0)
-    adj2[...] = mm(move, adj[...]).astype(BF)
-    loc2[...] = mm(move, loc[...].astype(BF))
-    cnt2[...] = mm(move, cnt.astype(BF))
+    ring_pass(0, table1, 1)
 
     drain(asked.at[pl.ds(1, ncol - 1)], req_recv)
 
@@ -319,13 +302,13 @@
         first, last = b * ROW // CAP, ((b + 1) * ROW - 1) // CAP
         reach.append((first * rows, (last + 1 - first) * rows))
 
-    @pl.loop(0, ncol)
-    def _(d):
-        got = asked[d]
-        spot = iota((ROW, LANES), 0) + lax.rem(d, 8) * ROW
-        for b in range(blocks):
-            first, deep = reach[b]
-            piece = jnp.broadcast_to(got[b], (ROW, LANES))
+    def pick_block(b):
+        first, deep = reach[b]
+
+        @pl.loop(0, ncol)
+        def _(d):
+            spot = iota((ROW, LANES), 0) + lax.rem(d, 8) * ROW
+            piece = jnp.broadcast_to(asked[d, b], (ROW, LANES))
             found = jnp.where(iota((ROW, LANES), 1) == spot, piece, 0)
             found = jnp.sum(found, axis=1, keepdims=True)
             hit = iota((ROW, deep), 1) + (first + 1) == found
@@ -362,16 +345,23 @@
                     cp.start()
 
     def serve_layer(layer, table, serve, ans):
-        serve_block(layer, table, serve, 0, (0,))
-        ring_wait(layer, table, 1, (1,))
-        ring_start(layer, table, 2, (1,))
-        serve_block(layer, table, serve, 0, (1,))
-        ring_wait(layer, table, 2)
-        ring_start(layer, table, 3)
-        ring_wait(layer, table, 3)
-        ring_start(layer, table, 4)
+        if layer == 0:
+            pick_block(0)
+            serve_block(layer, table, serve, 0, (0, 1))
+            ring_pass(layer, table, 2)
+            pick_block(1)
+            pick_block(2)
+        else:
+            ring_wait(layer, table, 1, (0,))
+            ring_start(layer, table, 2, (0,))
+            serve_block(layer, table, serve, 0, (0,))
+            ring_wait(layer, table, 1, (1,))
+            ring_start(layer, table, 2, (1,))
+            serve_block(layer, table, serve, 0, (1,))
+            ring_pass(layer, table, 2)
+        ring_pass(layer, table, 3)
         serve_block(layer, table, serve, 1, (0, 1))
-        ring_wait(layer, table, 4)
+        ring_pass(layer, table, 4)
         serve_block(layer, table, serve, 2, (0, 1))
         for b in range(blocks):
             ans[b, 0] = serve[b, 0]
@@ -382,10 +372,13 @@
             b, pl.ds(1, ncol - 1), :, pl.ds(halves[0] * wide, len(halves) * wide)
         ]
 
-    parts = ((0, (0,)), (0, (1,)), (1, (0, 1)), (2, (0, 1)))
+    parts = (
+        ((0, (0, 1)), (1, (0, 1)), (2, (0, 1))),
+        ((0, (0,)), (0, (1,)), (1, (0, 1)), (2, (0, 1))),
+    )
 
     def summed(layer, ans, b, adjacency):
-        for part in parts:
+        for part in parts[layer]:
             if part[0] == b:
                 drain(answers(ans, *part), ans_recv.at[layer, b, part[1][0]])
         return mm(
@@ -394,6 +387,28 @@
         )
 
     serve_layer(0, table1, serve1, ans1)
+    pos = pos_ref[...]
+    t_dev = pos // rows % n_dev
+    t_x = t_dev // (NZ * NC)
+    t_z = t_dev // NC % NZ
+    target = ((t_x + NX - me_x) % NX) * NZ + (t_z + NZ - me_z) % NZ
+    hot_t = iota((NX * NZ, rows), 0) == target
+    ahead_of = mm(one_zero(hot_t), sooner)
+    rank_t = jnp.sum(jnp.where(hot_t, ahead_of, 0.0), axis=0, keepdims=True)
+    move = one_zero(target * rank2 + rank_t.astype(jnp.int32) == sub)
+    pos_8 = jnp.broadcast_to((pos % rows).astype(F32), (16, rows)).astype(BF)
+    pos_t = lax.dot_general(
+        pos_8, move, (((1,), (1,)), ((), ())), preferred_element_type=F32
+    )
+    pos_out[...] = pos_t[0:8, :]
+    for d in range(1, NX * NZ):
+        send(pos_out, pos_in.at[d], pos_send, pos_recv, owner_at(d)).start()
+    pos_in[0] = pos_out[...]
+    adj[...] = one_zero(key_ref[...] > 0)
+    adj2[...] = mm(move, adj[...]).astype(BF)
+    loc2[...] = mm(move, loc[...].astype(BF))
+    cnt2[...] = mm(move, cnt.astype(BF))
+
     loads[1].wait()
     loads[2].wait()
     x = table1[own, :]
@@ -409,8 +424,6 @@
         table2[own, cols] = jnp.maximum(total, 0.0).astype(BF)
         ring_start(1, table2, 1, (h,))
     hid[...] = mm(move, table2[own, :]).astype(BF)
-    ring_wait(1, table2, 1, (0,))
-    ring_start(1, table2, 2, (0,))
     serve_layer(1, table2, serve2, ans2)
     loads[3].wait()
     loads[4].wait()
@@ -466,7 +479,7 @@
     drain(leave.at[pl.ds(1, 2 * pairs - 1)], out_send)
     for layer, table, serve in ((0, table1, serve1), (1, table2, serve2)):
         ring_left(layer, table)
-        for part in parts:
+        for part in parts[layer]:
             drain(answers(serve, *part), ans_send.at[layer, part[0], part[1][0]])
 
 

time: 120 us -> 117 us (0.975)
  Pallas kernels: 118 us -> 115 us
    pallas_call x1, Pallas kernels: 118 us -> 115 us  [body(): pl.pallas_call(kernel, out_shape=jax.ShapeDtypeStruct((rows, hidden), BF)...]
where the time goes in v4:
time: 117 us; the launch traced here: 116 us
  Pallas kernels  115 us (98%)
  local copies, waits for them, and re-layouts  1.67 us (1%)
    pallas_call x1, Pallas kernels, body(): pl.pallas_call(kernel, out_shape=jax.ShapeDtypeStruct((rows, hidden), BF)...  115 us

profile of v4, /device:TPU:1, one launch (start us, length us, event | category | flops | bytes accessed | tf_op | source)
XLA Modules:
  0.0 116.3 jit_solution(13547910936135419909)
XLA Ops:
  0.0 114.6 %shard_map.82 = bf16[128,1024]{1,0:T(8,128)(2,1)} custom-call(s32[25,128]{1,0:T(8,128)} %bitcast.3, s32[25,128]{1,0:T(8,128)} %bitcast.4, s32[1,128]{1,0:T(1,128)} %bitcast.5, bf16[128,768]{1,0:T(8,128)(2,1)} %feat_hbm.1, bf16[768,1024]{1,0:T(8,128)(2,1)} %ws1_hbm.1, bf16[768,1024]{1,0:T(8,128)(2,1)} %wn1_hbm.1, bf16[1024,1024]{1,0:T(8,128)(2,1)} %ws2_hbm.1, ...), custom_call_target="tpu_custom_call" | custom-call | tf_op jit(solution)/shard_map/pallas_call | solution.py:508
  114.6 1.7 %copy.10 = bf16[128,1024]{1,0:T(8,128)(2,1)} copy(bf16[128,1024]{1,0:T(8,128)(2,1)} %shard_map.82) | data formatting | bytes 524288

commit v5 on v4

--- a/solution.py
+++ b/solution.py
@@ -215,50 +215,6 @@
     diagonal = jnp.where(sub == lane, count, 0.0).astype(BF)
     cnt = mm(diagonal, ones)
 
-    loads[0].wait()
-    pl.semaphore_wait(barrier, len(peers))
-
-    def part_of(table, dz, h):
-        wide = table.shape[1] // 2
-        return table.at[pl.ds(place_of(dz) * rows, rows), pl.ds(h * wide, wide)]
-
-    def moves(s):
-        for way, sign in enumerate((-1, 1)):
-            for h in range(2):
-                if s < half or h == way:
-                    yield way, sign, h
-
-    def ring_start(layer, table, s, halves=(0, 1)):
-        for way, sign, h in moves(s):
-            if h in halves:
-                send(
-                    part_of(table, sign * (s - 1), h),
-                    part_of(table, sign * s, h),
-                    ring_send.at[layer, way, s - 1, h],
-                    ring_recv.at[layer, way, s - 1, h],
-                    along_z(1 if way == 0 else NZ - 1),
-                ).start()
-
-    def ring_wait(layer, table, s, halves=(0, 1)):
-        for way, sign, h in moves(s):
-            if h in halves:
-                drain(part_of(table, sign * s, h), ring_recv.at[layer, way, s - 1, h])
-
-    def ring_pass(layer, table, s):
-        for h in range(2):
-            ring_wait(layer, table, s, (h,))
-            if s < half:
-                ring_start(layer, table, s + 1, (h,))
-
-    def ring_left(layer, table):
-        for s in range(1, half + 1):
-            for way, sign, h in moves(s):
-                drain(
-                    part_of(table, sign * (s - 1), h), ring_send.at[layer, way, s - 1, h]
-                )
-
-    ring_start(0, table1, 1)
-
     tiles = ncol * block // LANES
     lists[...] = jnp.zeros_like(lists)
 
@@ -283,6 +239,50 @@
             near = near + jnp.where(row8[:, s : s + 1] == lane8, 1.0, 0.0)
         loc[at_rows, :] = near
 
+    loads[0].wait()
+    pl.semaphore_wait(barrier, len(peers))
+
+    def part_of(table, dz, h):
+        wide = table.shape[1] // 2
+        return table.at[pl.ds(place_of(dz) * rows, rows), pl.ds(h * wide, wide)]
+
+    def moves(s):
+        for way, sign in enumerate((-1, 1)):
+            for h in range(2):
+                if s < half or h == way:
+                    yield way, sign, h
+
+    def ring_start(layer, table, s, halves=(0, 1)):
+        for way, sign, h in moves(s):
+            if h in halves:
+                send(
+                    part_of(table, sign * (s - 1), h),
+                    part_of(table, sign * s, h),
+                    ring_send.at[layer, way, s - 1, h],
+                    ring_recv.at[layer, way, s - 1, h],
+                    along_z(1 if way == 0 else NZ - 1),
+                ).start()
+
+    def ring_wait(layer, table, s, halves=(0, 1)):
+        for way, sign, h in moves(s):
+            if h in halves:
+                drain(part_of(table, sign * s, h), ring_recv.at[layer, way, s - 1, h])
+
+    def ring_pass(layer, table, s):
+        for h in range(2):
+            ring_wait(layer, table, s, (h,))
+            if s < half:
+                ring_start(layer, table, s + 1, (h,))
+
+    def ring_left(layer, table):
+        for s in range(1, half + 1):
+            for way, sign, h in moves(s):
+                drain(
+                    part_of(table, sign * (s - 1), h), ring_send.at[layer, way, s - 1, h]
+                )
+
+    ring_start(0, table1, 1)
+
     window = blocks
     for d in range(1, ncol):
         send(
@@ -293,7 +293,6 @@
             behind(d),
         ).start()
     asked[0] = lists[0:window]
-    ring_pass(0, table1, 1)
 
     drain(asked.at[pl.ds(1, ncol - 1)], req_recv)
 
@@ -347,22 +346,20 @@
     def serve_layer(layer, table, serve, ans):
         if layer == 0:
             pick_block(0)
-            serve_block(layer, table, serve, 0, (0, 1))
-            ring_pass(layer, table, 2)
+        for h in range(2):
+            ring_wait(layer, table, 1, (h,))
+            ring_start(layer, table, 2, (h,))
+            serve_block(layer, table, serve, 0, (h,))
+        if layer == 0:
             pick_block(1)
+        ring_pass(layer, table, 2)
+        if layer == 0:
             pick_block(2)
-        else:
-            ring_wait(layer, table, 1, (0,))
-            ring_start(layer, table, 2, (0,))
-            serve_block(layer, table, serve, 0, (0,))
-            ring_wait(layer, table, 1, (1,))
-            ring_start(layer, table, 2, (1,))
-            serve_block(layer, table, serve, 0, (1,))
-            ring_pass(layer, table, 2)
         ring_pass(layer, table, 3)
         serve_block(layer, table, serve, 1, (0, 1))
         ring_pass(layer, table, 4)
-        serve_block(layer, table, serve, 2, (0, 1))
+        for h in range(2):
+            serve_block(layer, table, serve, 2, (h,))
         for b in range(blocks):
             ans[b, 0] = serve[b, 0]
 
@@ -372,21 +369,30 @@
             b, pl.ds(1, ncol - 1), :, pl.ds(halves[0] * wide, len(halves) * wide)
         ]
 
-    parts = (
-        ((0, (0, 1)), (1, (0, 1)), (2, (0, 1))),
-        ((0, (0,)), (0, (1,)), (1, (0, 1)), (2, (0, 1))),
-    )
-
-    def summed(layer, ans, b, adjacency):
-        for part in parts[layer]:
-            if part[0] == b:
-                drain(answers(ans, *part), ans_recv.at[layer, b, part[1][0]])
+    parts = ((0, (0,)), (0, (1,)), (1, (0, 1)), (2, (0,)), (2, (1,)))
+
+    def landed_sum(layer, ans, part, adjacency):
+        b, halves = part
+        wide = ans.shape[3] // 2
+        cols = slice(halves[0] * wide, (halves[-1] + 1) * wide)
+        drain(answers(ans, b, halves), ans_recv.at[layer, b, halves[0]])
         return mm(
             adjacency[:, b * per_block : (b + 1) * per_block],
-            ans[b].reshape(per_block, ans.shape[3]),
+            ans[b, :, :, cols].reshape(per_block, len(halves) * wide),
         )
 
+    def means(layer, ans, near, adjacency, degrees):
+        wide = ans.shape[3] // 2
+        sums = [near[:, h * wide : (h + 1) * wide] for h in range(2)]
+        for part in parts:
+            got = landed_sum(layer, ans, part, adjacency)
+            for k, h in enumerate(part[1]):
+                sums[h] = sums[h] + got[:, k * wide : (k + 1) * wide]
+            if part[0] == blocks - 1:
+                yield slice(h * wide, (h + 1) * wide), (sums[h] / degrees).astype(BF)
+
     serve_layer(0, table1, serve1, ans1)
+
     pos = pos_ref[...]
     t_dev = pos // rows % n_dev
     t_x = t_dev // (NZ * NC)
@@ -413,14 +419,15 @@
     loads[2].wait()
     x = table1[own, :]
     acc[...] = mm(x, ws1[...])
-    total = mm(loc[...].astype(BF), x)
-    for b in range(blocks):
-        total = total + summed(0, ans1, b, adj)
-    m = (total / cnt[:, 0:1]).astype(BF)
+    near = mm(loc[...].astype(BF), x)
+    halves1 = means(0, ans1, near, adj, cnt[:, 0:1])
+    rows_of, m = next(halves1)
+    acc[...] += mm(m, wn1[rows_of, :])
+    rows_of, m = next(halves1)
     wide = hidden_width // 2
     for h in range(2):
         cols = slice(h * wide, (h + 1) * wide)
-        total = acc[:, cols] + mm(m, wn1[:, cols])
+        total = acc[:, cols] + mm(m, wn1[rows_of, cols])
         table2[own, cols] = jnp.maximum(total, 0.0).astype(BF)
         ring_start(1, table2, 1, (h,))
     hid[...] = mm(move, table2[own, :]).astype(BF)
@@ -429,11 +436,9 @@
     loads[4].wait()
     acc[...] = mm(hid[...], ws2[...])
     drain(pos_in.at[pl.ds(1, NX * NZ - 1)], pos_recv)
-    total = mm(loc2[...].astype(BF), table2[own, :])
-    for b in range(blocks):
-        total = total + summed(1, ans2, b, adj2)
-    m = (total / cnt2[:, 0:1]).astype(BF)
-    acc[...] += mm(m, wn2[...])
+    near = mm(loc2[...].astype(BF), table2[own, :])
+    for rows_of, m in means(1, ans2, near, adj2, cnt2[:, 0:1]):
+        acc[...] += mm(m, wn2[rows_of, :])
 
     fold_rows = 2 * rank2
     pairs = NX * NZ // 2
@@ -479,7 +484,7 @@
     drain(leave.at[pl.ds(1, 2 * pairs - 1)], out_send)
     for layer, table, serve in ((0, table1, serve1), (1, table2, serve2)):
         ring_left(layer, table)
-        for part in parts[layer]:
+        for part in parts:
             drain(answers(serve, *part), ans_send.at[layer, part[0], part[1][0]])
 
 

time: 117 us -> 120 us (1.026)
  Pallas kernels: 115 us -> 118 us
    pallas_call x1, Pallas kernels: 115 us -> 118 us  [body(): pl.pallas_call(kernel, out_shape=jax.ShapeDtypeStruct((rows, hidden), BF)...]
where the time goes in v5:
time: 120 us; the launch traced here: 119 us
  Pallas kernels  118 us (98%)
  local copies, waits for them, and re-layouts  1.67 us (1%)
    pallas_call x1, Pallas kernels, body(): pl.pallas_call(kernel, out_shape=jax.ShapeDtypeStruct((rows, hidden), BF)...  118 us

profile of v5, /device:TPU:1, one launch (start us, length us, event | category | flops | bytes accessed | tf_op | source)
XLA Modules:
  0.0 119.5 jit_solution(1778879514318910184)
XLA Ops:
  0.0 117.8 %shard_map.82 = bf16[128,1024]{1,0:T(8,128)(2,1)} custom-call(s32[25,128]{1,0:T(8,128)} %bitcast.3, s32[25,128]{1,0:T(8,128)} %bitcast.4, s32[1,128]{1,0:T(1,128)} %bitcast.5, bf16[128,768]{1,0:T(8,128)(2,1)} %feat_hbm.1, bf16[768,1024]{1,0:T(8,128)(2,1)} %ws1_hbm.1, bf16[768,1024]{1,0:T(8,128)(2,1)} %wn1_hbm.1, bf16[1024,1024]{1,0:T(8,128)(2,1)} %ws2_hbm.1, ...), custom_call_target="tpu_custom_call" | custom-call | tf_op jit(solution)/shard_map/pallas_call | solution.py:513
  117.8 1.7 %copy.10 = bf16[128,1024]{1,0:T(8,128)(2,1)} copy(bf16[128,1024]{1,0:T(8,128)(2,1)} %shard_map.82) | data formatting | bytes 524288

commit v6 on v4

--- a/solution.py
+++ b/solution.py
@@ -320,8 +320,9 @@
         wide = table.shape[1] // 2
         at_col, n_col = halves[0] * wide, len(halves) * wide
 
-        @pl.loop(0, NX)
-        def _(j):
+        @pl.loop(1, NX + 1)
+        def _(turn):
+            j = lax.rem(turn, NX)
             some = pl.ds(pl.multiple_of(j * plane * ROW, plane * ROW), plane * ROW)
             picked = mm(
                 pick[b, some, 0:deep],
@@ -350,7 +351,6 @@
             serve_block(layer, table, serve, 0, (0, 1))
             ring_pass(layer, table, 2)
             pick_block(1)
-            pick_block(2)
         else:
             ring_wait(layer, table, 1, (0,))
             ring_start(layer, table, 2, (0,))
@@ -361,6 +361,8 @@
             ring_pass(layer, table, 2)
         ring_pass(layer, table, 3)
         serve_block(layer, table, serve, 1, (0, 1))
+        if layer == 0:
+            pick_block(2)
         ring_pass(layer, table, 4)
         serve_block(layer, table, serve, 2, (0, 1))
         for b in range(blocks):

time: 117 us -> 117 us (level)
  no operation moved by 1% of the time
where the time goes in v6:
time: 117 us; the launch traced here: 116 us
  Pallas kernels  114 us (97%)
  local copies, waits for them, and re-layouts  1.67 us (1%)
    pallas_call x1, Pallas kernels, body(): pl.pallas_call(kernel, out_shape=jax.ShapeDtypeStruct((rows, hidden), BF)...  114 us

profile of v6, /device:TPU:1, one launch (start us, length us, event | category | flops | bytes accessed | tf_op | source)
XLA Modules:
  0.0 116.1 jit_solution(1113993615260442526)
XLA Ops:
  0.0 114.4 %shard_map.82 = bf16[128,1024]{1,0:T(8,128)(2,1)} custom-call(s32[25,128]{1,0:T(8,128)} %bitcast.3, s32[25,128]{1,0:T(8,128)} %bitcast.4, s32[1,128]{1,0:T(1,128)} %bitcast.5, bf16[128,768]{1,0:T(8,128)(2,1)} %feat_hbm.1, bf16[768,1024]{1,0:T(8,128)(2,1)} %ws1_hbm.1, bf16[768,1024]{1,0:T(8,128)(2,1)} %wn1_hbm.1, bf16[1024,1024]{1,0:T(8,128)(2,1)} %ws2_hbm.1, ...), custom_call_target="tpu_custom_call" | custom-call | tf_op jit(solution)/shard_map/pallas_call | solution.py:510
  114.4 1.7 %copy.10 = bf16[128,1024]{1,0:T(8,128)(2,1)} copy(bf16[128,1024]{1,0:T(8,128)(2,1)} %shard_map.82) | data formatting | bytes 524288

commit v7 on v6

--- a/solution.py
+++ b/solution.py
@@ -348,8 +348,8 @@
     def serve_layer(layer, table, serve, ans):
         if layer == 0:
             pick_block(0)
+            ring_pass(layer, table, 2)
             serve_block(layer, table, serve, 0, (0, 1))
-            ring_pass(layer, table, 2)
             pick_block(1)
         else:
             ring_wait(layer, table, 1, (0,))

time: 117 us -> 116 us (level)
  no operation moved by 1% of the time
where the time goes in v7:
time: 116 us
  Pallas kernels  114 us (98%)
  local copies, waits for them, and re-layouts  1.67 us (1%)
    pallas_call x1, Pallas kernels, body(): pl.pallas_call(kernel, out_shape=jax.ShapeDtypeStruct((rows, hidden), BF)...  114 us

profile of v7, /device:TPU:1, one launch (start us, length us, event | category | flops | bytes accessed | tf_op | source)
XLA Modules:
  0.0 116.0 jit_solution(7903179488152573435)
XLA Ops:
  0.0 114.3 %shard_map.82 = bf16[128,1024]{1,0:T(8,128)(2,1)} custom-call(s32[25,128]{1,0:T(8,128)} %bitcast.3, s32[25,128]{1,0:T(8,128)} %bitcast.4, s32[1,128]{1,0:T(1,128)} %bitcast.5, bf16[128,768]{1,0:T(8,128)(2,1)} %feat_hbm.1, bf16[768,1024]{1,0:T(8,128)(2,1)} %ws1_hbm.1, bf16[768,1024]{1,0:T(8,128)(2,1)} %wn1_hbm.1, bf16[1024,1024]{1,0:T(8,128)(2,1)} %ws2_hbm.1, ...), custom_call_target="tpu_custom_call" | custom-call | tf_op jit(solution)/shard_map/pallas_call | solution.py:510
  114.3 1.7 %copy.10 = bf16[128,1024]{1,0:T(8,128)(2,1)} copy(bf16[128,1024]{1,0:T(8,128)(2,1)} %shard_map.82) | data formatting | bytes 524288
